TPU v7x, 128 devices: a whole 4x4x4 slice. The times are simulated.
128 devices in a mesh: section: 8 (over y_lo, x), expert: 16 (over y_hi, z, core).
Axes of the slice: x: 4, y: 4 (y_hi: 2, y_lo: 2; y = y_hi * 2 + y_lo), z: 4, core: 2. Of those that a mesh axis runs over, the one named last changes fastest.
Arguments:
- fwd_acts: bfloat16 [8, 2048, 3584], P('section', 'expert'), may hold values from -6 to 6
- bwd_saved: bfloat16 [8, 2048, 3584], P('section', 'expert'), may hold values from -6 to 6
- bwd_cot: bfloat16 [8, 2048, 3584], P('section', 'expert'), may hold values from -6 to 6
- fwd_ids: int32 [8, 2048, 2], P('section', 'expert'), may hold values from 0 to 15, all different within a row; in each aligned block of 128 rows (0 to 127, 128 to 255, ..., all dimensions but the last counted through in order) at most 20 rows name the same one
- bwd_ids: int32 [8, 2048, 2], P('section', 'expert'), may hold values from 0 to 15, all different within a row; in each aligned block of 128 rows (0 to 127, 128 to 255, ..., all dimensions but the last counted through in order) at most 20 rows name the same one
- norm_gain: bfloat16 [8, 3584], P('section'), may hold values from 0.099609375 to 1.8984375
- router: bfloat16 [8, 3584, 16], P('section'), may hold values from -0.09375 to 0.09375
- w_gate: bfloat16 [8, 16, 3584, 1024], P('section', 'expert'), may hold values from -0.09375 to 0.09375
- w_up: bfloat16 [8, 16, 3584, 1024], P('section', 'expert'), may hold values from -0.09375 to 0.09375
- w_down: bfloat16 [8, 16, 1024, 3584], P('section', 'expert'), may hold values from -0.1875 to 0.1875
Outputs:
- fwd_out: bfloat16 [8, 2048, 3584], P('section', 'expert')
- bwd_grad: bfloat16 [8, 2048, 3584], P('section', 'expert')
Inputs may be any that keep to these rules, and one draw needn't show every extreme that they name: `fwd_ids`: each token names 2 different experts; in each aligned block of 128 rows (the rows of one device) no expert is named by more than 20 rows, a bound that some block reaches. `bwd_ids`: each token names 2 different experts; in each aligned block of 128 rows (the rows of one device) no expert is named by more than 20 rows, a bound that some block reaches.
All inputs are finite; a program needn't handle non-finite values.
Results may differ from a plain program's by a relative error of at most 0.0066.
Values may be sent and summed in bfloat16 or wider, within the bound.
A program may use at most 128 MiB of HBM per device.

v0:
```python
import jax
import jax.numpy as jnp
from jax import lax
from jax.sharding import PartitionSpec as P

route_scale = 2.5
epsilon = 1e-06


def from_behind(value, axis, steps):
    count = lax.axis_size(axis)
    pairs = [(source, (source + steps) % count) for source in range(count)]
    return lax.ppermute(value, axis, pairs)


def normalize(x, gain):
    xf = x.astype(jnp.float32)
    inv = lax.rsqrt(jnp.mean(xf * xf, axis=-1, keepdims=True) + epsilon)
    normed = (xf * inv * gain.astype(jnp.float32)).astype(jnp.bfloat16)
    return (xf, inv, normed)


def gating(normed, route_w, ids):
    logits = jnp.dot(normed, route_w, preferred_element_type=jnp.float32)
    count = route_w.shape[-1]
    hot = (ids[:, :, None] == jnp.arange(count, dtype=jnp.int32)[None, None, :]).astype(jnp.float32)
    chosen = jnp.sum(hot * logits[:, None, :], axis=-1)
    score = jax.nn.sigmoid(chosen)
    total = jnp.sum(score, axis=-1, keepdims=True)
    weight = route_scale * score / total
    return (hot, score, total, weight)


def routing_picks(ids, experts, capacity):
    hot = (ids[:, :, None] == jnp.arange(experts, dtype=jnp.int32)[None, None, :]).astype(jnp.int32)
    flat = hot.reshape(-1, experts)
    before = jnp.cumsum(flat, axis=0) - flat
    slots = jnp.sum(before * flat, axis=-1).reshape(ids.shape)
    target = ids * capacity + slots
    return (
        target[:, :, None] == jnp.arange(experts * capacity, dtype=jnp.int32)[None, None, :]
    ).astype(jnp.bfloat16)


def dispatch(picks, rows, experts, capacity):
    placed = jnp.einsum("tkr,td->rd", picks, rows, preferred_element_type=jnp.float32)
    return placed.astype(jnp.bfloat16).reshape(experts, capacity, rows.shape[-1])


def collect(picks, returned):
    flat = returned.reshape(-1, returned.shape[-1])
    return jnp.einsum("tkr,rd->tkd", picks, flat, preferred_element_type=jnp.float32)


def expert_forward(rows, wg, wu, wd):
    gate = jnp.dot(rows, wg, preferred_element_type=jnp.float32)
    upper = jnp.dot(rows, wu, preferred_element_type=jnp.float32)
    act = (gate * jax.nn.sigmoid(gate) * upper).astype(jnp.bfloat16)
    return jnp.dot(act, wd, preferred_element_type=jnp.float32).astype(jnp.bfloat16)


def expert_backward(rows, cot, wg, wu, wd):
    gate = jnp.dot(rows, wg, preferred_element_type=jnp.float32)
    upper = jnp.dot(rows, wu, preferred_element_type=jnp.float32)
    sig = jax.nn.sigmoid(gate)
    act = (gate * sig * upper).astype(jnp.bfloat16)
    output = jnp.dot(act, wd, preferred_element_type=jnp.float32).astype(jnp.bfloat16)
    grad_act = jnp.dot(cot, wd.T, preferred_element_type=jnp.float32)
    dgate = (grad_act * upper * sig * (1.0 + gate * (1.0 - sig))).astype(jnp.bfloat16)
    dup = (grad_act * gate * sig).astype(jnp.bfloat16)
    unit = jnp.dot(dgate, wg.T, preferred_element_type=jnp.float32) + jnp.dot(
        dup, wu.T, preferred_element_type=jnp.float32
    )
    return (unit.astype(jnp.bfloat16), output)


def per_device(
    fwd_acts, bwd_saved, bwd_cot, fwd_ids, bwd_ids, norm_gain, router, w_gate, w_up, w_down
):
    width = fwd_acts.shape[-1]
    experts = router.shape[-1]
    tok_dev = fwd_acts.shape[1]
    top = fwd_ids.shape[-1]
    capacity = 5 * tok_dev * top // (4 * experts)
    arrive_f = from_behind(fwd_acts, "section", 1)[0]
    arrive_b = from_behind(bwd_cot, "section", -1)[0]
    gain = norm_gain[0]
    route_w = router[0]
    wg = w_gate[0, 0]
    wu = w_up[0, 0]
    wd = w_down[0, 0]
    xf, inv_f, normed_f = normalize(arrive_f, gain)
    hot_f, score_f, total_f, weight_f = gating(normed_f, route_w, fwd_ids[0])
    picks_f = routing_picks(fwd_ids[0], experts, capacity)
    send_f = dispatch(picks_f, normed_f, experts, capacity)
    xb, inv_b, normed_b = normalize(bwd_saved[0], gain)
    hot_b, score_b, total_b, weight_b = gating(normed_b, route_w, bwd_ids[0])
    picks_b = routing_picks(bwd_ids[0], experts, capacity)
    send_n = dispatch(picks_b, normed_b, experts, capacity)
    send_c = dispatch(picks_b, arrive_b, experts, capacity)
    items = lax.all_to_all(send_f, "expert", split_axis=0, concat_axis=0, tiled=True)
    rows = items.reshape(-1, width)
    out_f = lax.all_to_all(
        expert_forward(rows, wg, wu, wd).reshape(items.shape),
        "expert",
        split_axis=0,
        concat_axis=0,
        tiled=True,
    )
    items_n = lax.all_to_all(send_n, "expert", split_axis=0, concat_axis=0, tiled=True)
    rows_c = lax.all_to_all(send_c, "expert", split_axis=0, concat_axis=0, tiled=True).reshape(
        -1, width
    )
    unit, output = expert_backward(items_n.reshape(-1, width), rows_c, wg, wu, wd)
    extra = output.reshape(items_n.shape)
    unit_part = unit.reshape(items_n.shape)
    unit_ret = lax.all_to_all(unit_part, "expert", split_axis=0, concat_axis=0, tiled=True)
    extra_ret = lax.all_to_all(extra, "expert", split_axis=0, concat_axis=0, tiled=True)
    mixed = jnp.sum(weight_f[..., None] * collect(picks_f, out_f), axis=1)
    fwd_out = (xf + mixed).astype(jnp.bfloat16)
    cot_f = arrive_b.astype(jnp.float32)
    from_experts = jnp.sum(weight_b[..., None] * collect(picks_b, unit_ret), axis=1)
    outputs_k = collect(picks_b, extra_ret)
    product = jnp.sum(outputs_k * cot_f[:, None, :], axis=-1)
    product = lax.optimization_barrier(product.astype(jnp.bfloat16)).astype(jnp.float32)
    dscore = (
        route_scale
        / total_b
        * (product - jnp.sum(product * weight_b, axis=-1, keepdims=True) / route_scale)
    )
    dlogit = dscore * score_b * (1.0 - score_b)
    dlogits = jnp.sum(hot_b * dlogit[..., None], axis=1).astype(jnp.bfloat16)
    dnormed = from_experts + jnp.dot(dlogits, route_w.T, preferred_element_type=jnp.float32)
    scaled = gain.astype(jnp.float32) * dnormed
    dx = inv_b * scaled - xb * inv_b**3 * jnp.mean(xb * scaled, axis=-1, keepdims=True)
    bwd_grad = (cot_f + dx).astype(jnp.bfloat16)
    return (fwd_out[None], bwd_grad[None])


def solution(mesh):
    return jax.shard_map(
        per_device,
        mesh=mesh,
        in_specs=(
            P("section", "expert", None),
            P("section", "expert", None),
            P("section", "expert", None),
            P("section", "expert", None),
            P("section", "expert", None),
            P("section", None),
            P("section", None, None),
            P("section", "expert", None, None),
            P("section", "expert", None, None),
            P("section", "expert", None, None),
        ),
        out_specs=(P("section", "expert", None), P("section", "expert", None)),
        check_vma=False,
    )
```

profile of v0, /device:TPU:1, one launch (start us, length us, event | category | flops | bytes accessed | tf_op | source)
XLA Modules:
  0.0 313.2 jit_solution(17738828399186920163)
XLA Ops:
  8.9 9.6 %all-to-all-start.3 = ((bf16[16,20,3584]{2,1,0:T(8,128)(2,1)}), bf16[16,20,3584]{2,1,0:T(8,128)(2,1)}, u32[]{:S(2)}, u32[]{:S(2)}) async-start(bf16[16,20,3584]{2,1,0:T(8,128)(2,1)} %reshape.234), calls=%async_computation.3 | async-start | bytes 5505024 | tf_op jit(solution)/shard_map/all_to_all | solution.py:110
  23.5 17.4 %collective-permute-done.1 = bf16[1,128,3584]{2,1,0:T(8,128)(2,1)} collective-permute-done((bf16[1,128,3584]{2,1,0:T(8,128)(2,1)S(1)}, bf16[1,128,3584]{2,1,0:T(8,128)(2,1)}, u32[]{:S(2)}, u32[]{:S(2)}) %collective-permute-start.1) | collective-permute-done | bytes 917536 | tf_op jit(solution)/shard_map/ppermute | solution.py:13
  45.0 28.8 %all-to-all-done.3 = bf16[16,20,3584]{2,1,0:T(8,128)(2,1)} async-done(((bf16[16,20,3584]{2,1,0:T(8,128)(2,1)}), bf16[16,20,3584]{2,1,0:T(8,128)(2,1)}, u32[]{:S(2)}, u32[]{:S(2)}) %all-to-all-start.3) | async-done | bytes 2293792 | tf_op jit(solution)/shard_map/all_to_all | solution.py:110
  73.8 8.1 %all-to-all-start.2 = ((bf16[16,20,3584]{2,1,0:T(8,128)(2,1)}), bf16[16,20,3584]{2,1,0:T(8,128)(2,1)}, u32[]{:S(2)}, u32[]{:S(2)}) async-start(bf16[16,20,3584]{2,1,0:T(8,128)(2,1)} %reshape.232), calls=%async_computation.2 | async-start | bytes 5505024 | tf_op jit(solution)/shard_map/all_to_all | solution.py:111
  90.7 4.1 %reshape.235 = bf16[320,3584]{1,0:T(8,128)(2,1)} reshape(bf16[16,20,3584]{2,1,0:T(8,128)(2,1)} %all-to-all-done.3) | data formatting | bytes 4587520 | tf_op jit(solution)/shard_map/reshape | solution.py:114
  94.9 23.3 %all-to-all-done.2 = bf16[16,20,3584]{2,1,0:T(8,128)(2,1)} async-done(((bf16[16,20,3584]{2,1,0:T(8,128)(2,1)}), bf16[16,20,3584]{2,1,0:T(8,128)(2,1)}, u32[]{:S(2)}, u32[]{:S(2)}) %all-to-all-start.2) | async-done | bytes 2293792 | tf_op jit(solution)/shard_map/all_to_all | solution.py:111
  118.2 9.4 %all-to-all-start = ((bf16[16,20,3584]{2,1,0:T(8,128)(2,1)}), bf16[16,20,3584]{2,1,0:T(8,128)(2,1)}, u32[]{:S(2)}, u32[]{:S(2)}) async-start(bf16[16,20,3584]{2,1,0:T(8,128)(2,1)} %reshape.226), calls=%async_computation | async-start | bytes 5505024 | tf_op jit(solution)/shard_map/all_to_all | solution.py:101
  127.6 6.4 %fusion.14 = f32[320,1024]{1,0:T(8,128)S(1)} fusion(bf16[320,3584]{1,0:T(8,128)(2,1)} %reshape.235, bf16[1,1,3584,1024]{3,2,1,0:T(8,128)(2,1)} %param.17), kind=kOutput, calls=%fused_computation.14 | convolution fusion | flops 2348810240 | bytes 10944512 | tf_op jit(solution)/shard_map/dot_general | solution.py:63
  134.1 6.2 %fusion.8 = f32[320,1024]{1,0:T(8,128)S(1)} fusion(bf16[320,3584]{1,0:T(8,128)(2,1)S(1)} %copy-done.2, bf16[1,1,3584,1024]{3,2,1,0:T(8,128)(2,1)} %param.18), kind=kOutput, calls=%fused_computation.8 | convolution fusion | flops 2348810240 | bytes 10944512 | tf_op jit(solution)/shard_map/dot_general | solution.py:64
  141.4 7.2 %fusion.27 = bf16[320,3584]{1,0:T(8,128)(2,1)} fusion(bf16[1,1,1024,3584]{3,2,1,0:T(8,128)(2,1)} %param.19, f32[320,1024]{1,0:T(8,128)S(1)} %fusion.8, f32[320,1024]{1,0:T(8,128)S(1)} %fusion.14), kind=kOutput, calls=%fused_computation.23 | convolution fusion | flops 2351923200 | bytes 12255232 | tf_op jit(solution)/shard_map/dot_general | solution.py:67
  148.5 4.1 %reshape.238 = bf16[16,20,3584]{2,1,0:T(8,128)(2,1)} reshape(bf16[320,3584]{1,0:T(8,128)(2,1)} %fusion.27) | data formatting | bytes 4587520 | tf_op jit(solution)/shard_map/reshape | solution.py:115
  152.7 4.1 %reshape.233 = bf16[320,3584]{1,0:T(8,128)(2,1)} reshape(bf16[16,20,3584]{2,1,0:T(8,128)(2,1)} %all-to-all-done.2) | data formatting | bytes 4587520 | tf_op jit(solution)/shard_map/reshape | solution.py:111
  156.8 7.1 %all-to-all-done = bf16[16,20,3584]{2,1,0:T(8,128)(2,1)} async-done(((bf16[16,20,3584]{2,1,0:T(8,128)(2,1)}), bf16[16,20,3584]{2,1,0:T(8,128)(2,1)}, u32[]{:S(2)}, u32[]{:S(2)}) %all-to-all-start) | async-done | bytes 2293792 | tf_op jit(solution)/shard_map/all_to_all | solution.py:101
  163.9 9.4 %all-to-all-start.5 = ((bf16[16,20,3584]{2,1,0:T(8,128)(2,1)}), bf16[16,20,3584]{2,1,0:T(8,128)(2,1)}, u32[]{:S(2)}, u32[]{:S(2)}) async-start(bf16[16,20,3584]{2,1,0:T(8,128)(2,1)} %reshape.238), calls=%async_computation.5 | async-start | bytes 5505024 | tf_op jit(solution)/shard_map/all_to_all | solution.py:118
  173.3 6.5 %fusion.2 = f32[320,1024]{1,0:T(8,128)S(1)} fusion(bf16[320,3584]{1,0:T(8,128)(2,1)} %reshape.233, bf16[1,1,1024,3584]{3,2,1,0:T(8,128)(2,1)} %param.19), kind=kOutput, calls=%fused_computation.2 | convolution fusion | flops 2348810240 | bytes 10944512 | tf_op jit(solution)/shard_map/dot_general | solution.py:68
  179.8 5.9 %fusion.6 = f32[320,3584]{1,0:T(8,128)S(1)} fusion(bf16[1,1,3584,1024]{3,2,1,0:T(8,128)(2,1)} %param.18, f32[320,1024]{1,0:T(8,128)S(1)} %fusion.2, f32[320,1024]{1,0:T(8,128)S(1)} %copy-done.15), kind=kOutput, calls=%fused_computation.6 | convolution fusion | flops 2350776320 | bytes 14548992 | tf_op jit(solution)/shard_map/dot_general | solution.py:71
  185.7 4.3 %fusion.21 = bf16[320,3584]{1,0:T(8,128)(2,1)} fusion(f32[320,3584]{1,0:T(8,128)S(1)} %fusion.6, bf16[1,1,3584,1024]{3,2,1,0:T(8,128)(2,1)S(1)} %bitcast.159, f32[320,1024]{1,0:T(8,128)S(1)} %copy-done.15, f32[320,1024]{1,0:T(8,128)S(1)} %fusion.2, f32[320,1024]{1,0:T(8,128)S(1)} %copy-done.17), kind=kOutput, calls=%fused_computation.21 | convolution fusion | flops 2354380800 | bytes 18153472 | tf_op jit(solution)/shard_map/dot_general | solution.py:71
  190.0 4.2 %reshape.236 = bf16[16,20,3584]{2,1,0:T(8,128)(2,1)} reshape(bf16[320,3584]{1,0:T(8,128)(2,1)} %fusion.21) | data formatting | bytes 4587520 | tf_op jit(solution)/shard_map/reshape | solution.py:116
  194.2 4.1 %reshape.227 = bf16[320,3584]{1,0:T(8,128)(2,1)} reshape(bf16[16,20,3584]{2,1,0:T(8,128)(2,1)} %all-to-all-done) | data formatting | bytes 4587520 | tf_op jit(solution)/shard_map/reshape | solution.py:102
  198.4 11.3 %all-to-all-done.5 = bf16[16,20,3584]{2,1,0:T(8,128)(2,1)} async-done(((bf16[16,20,3584]{2,1,0:T(8,128)(2,1)}), bf16[16,20,3584]{2,1,0:T(8,128)(2,1)}, u32[]{:S(2)}, u32[]{:S(2)}) %all-to-all-start.5) | async-done | bytes 2293792 | tf_op jit(solution)/shard_map/all_to_all | solution.py:118
  209.6 9.4 %all-to-all-start.4 = ((bf16[16,20,3584]{2,1,0:T(8,128)(2,1)}), bf16[16,20,3584]{2,1,0:T(8,128)(2,1)}, u32[]{:S(2)}, u32[]{:S(2)}) async-start(bf16[16,20,3584]{2,1,0:T(8,128)(2,1)} %reshape.236), calls=%async_computation.4 | async-start | bytes 5505024 | tf_op jit(solution)/shard_map/all_to_all | solution.py:117
  219.0 7.4 %fusion.16 = f32[320,1024]{1,0:T(8,128)} fusion(bf16[320,3584]{1,0:T(8,128)(2,1)} %reshape.227, bf16[1,1,3584,1024]{3,2,1,0:T(8,128)(2,1)} %param.17), kind=kOutput, calls=%fused_computation.16 | convolution fusion | flops 2348810240 | bytes 10944512 | tf_op jit(solution)/shard_map/dot_general | solution.py:56
  226.4 12.5 %fusion.24 = bf16[320,3584]{1,0:T(8,128)(2,1)} fusion(bf16[1,1,1024,3584]{3,2,1,0:T(8,128)(2,1)} %param.19, bf16[320,3584]{1,0:T(8,128)(2,1)} %reshape.227, bf16[1,1,3584,1024]{3,2,1,0:T(8,128)(2,1)} %param.18, f32[320,1024]{1,0:T(8,128)} %fusion.16), kind=kOutput, calls=%fused_computation.22 | convolution fusion | flops 4700733440 | bytes 20578304 | tf_op jit(solution)/shard_map/dot_general | solution.py:59
  238.9 4.1 %reshape.228 = bf16[16,20,3584]{2,1,0:T(8,128)(2,1)} reshape(bf16[320,3584]{1,0:T(8,128)(2,1)} %fusion.24) | data formatting | bytes 4587520 | tf_op jit(solution)/shard_map/reshape | solution.py:104
  243.1 12.3 %all-to-all-done.4 = bf16[16,20,3584]{2,1,0:T(8,128)(2,1)} async-done(((bf16[16,20,3584]{2,1,0:T(8,128)(2,1)}), bf16[16,20,3584]{2,1,0:T(8,128)(2,1)}, u32[]{:S(2)}, u32[]{:S(2)}) %all-to-all-start.4) | async-done | bytes 2293792 | tf_op jit(solution)/shard_map/all_to_all | solution.py:117
  255.3 9.4 %all-to-all-start.1 = ((bf16[16,20,3584]{2,1,0:T(8,128)(2,1)}), bf16[16,20,3584]{2,1,0:T(8,128)(2,1)}, u32[]{:S(2)}, u32[]{:S(2)}) async-start(bf16[16,20,3584]{2,1,0:T(8,128)(2,1)} %reshape.228), calls=%async_computation.1 | async-start | bytes 5505024 | tf_op jit(solution)/shard_map/all_to_all | solution.py:103
  264.7 4.1 %reshape.245 = bf16[320,3584,1]{1,0,2:T(8,128)(2,1)} reshape(bf16[16,20,3584]{2,1,0:T(8,128)(2,1)} %all-to-all-done.5) | data formatting | bytes 4587520 | tf_op jit(solution)/shard_map/reshape | solution.py:51
  268.9 2.9 multiply_reduce_fusion
  271.8 2.7 reshape.244
  276.4 24.7 %all-to-all-done.1 = bf16[16,20,3584]{2,1,0:T(8,128)(2,1)} async-done(((bf16[16,20,3584]{2,1,0:T(8,128)(2,1)}), bf16[16,20,3584]{2,1,0:T(8,128)(2,1)}, u32[]{:S(2)}, u32[]{:S(2)}) %all-to-all-start.1) | async-done | bytes 2293792 | tf_op jit(solution)/shard_map/all_to_all | solution.py:103
  301.0 4.1 %reshape.243 = bf16[320,3584,1]{1,0,2:T(8,128)(2,1)} reshape(bf16[16,20,3584]{2,1,0:T(8,128)(2,1)} %all-to-all-done.1) | data formatting | bytes 4587520 | tf_op jit(solution)/shard_map/reshape | solution.py:51
  305.2 3.0 fusion.53
  (100 shorter events, 34.0 us)
Async XLA Ops:
  0.6 22.3 %copy-start = (bf16[1,3584,16]{1,2,0:T(8,128)(2,1)S(1)}, bf16[1,3584,16]{1,2,0:T(8,128)(2,1)}, u32[]{:S(2)}) copy-start(bf16[1,3584,16]{1,2,0:T(8,128)(2,1)} %param.16) | copy-start | bytes 344068
  0.6 5.2 %copy-start.1 = (bf16[1,128,3584]{2,1,0:T(8,128)(2,1)S(1)}, bf16[1,128,3584]{2,1,0:T(8,128)(2,1)}, u32[]{:S(2)}) copy-start(bf16[1,128,3584]{2,1,0:T(8,128)(2,1)} %param.11) | copy-start | bytes 2752516
  3.0 2.9 copy-start.5
  3.8 19.1 %copy-start.3 = (f32[3584]{0:T(1024)}, f32[3584]{0:T(1024)S(1)}, u32[]{:S(2)}) copy-start(f32[3584]{0:T(1024)S(1)} %convert_reduce_fusion.2) | copy-start | bytes 43012
  5.9 17.1 %copy-start.9 = (f32[128]{0:T(128)}, f32[128]{0:T(128)S(1)}, u32[]{:S(2)}) copy-start(f32[128]{0:T(128)S(1)} %get-tuple-element.9) | copy-start | bytes 1540
  8.9 9.6 %copy-start.13 = (bf16[1,128,3584]{2,1,0:T(8,128)(2,1)S(1)}, bf16[1,128,3584]{2,1,0:T(8,128)(2,1)}, u32[]{:S(2)}) copy-start(bf16[1,128,3584]{2,1,0:T(8,128)(2,1)} %param.12) | copy-start | bytes 2752516
  8.9 12.3 %copy-start.11 = (s32[1,128,2]{1,2,0:T(2,128)S(1)}, s32[1,128,2]{1,2,0:T(2,128)}, u32[]{:S(2)}) copy-start(s32[1,128,2]{1,2,0:T(2,128)} %param.13) | copy-start | bytes 3076
  8.9 64.8 %all-to-all-start.3 = ((bf16[16,20,3584]{2,1,0:T(8,128)(2,1)}), bf16[16,20,3584]{2,1,0:T(8,128)(2,1)}, u32[]{:S(2)}, u32[]{:S(2)}) async-start(bf16[16,20,3584]{2,1,0:T(8,128)(2,1)} %reshape.234), calls=%async_computation.3 | async-start | bytes 5505024 | tf_op jit(solution)/shard_map/all_to_all | solution.py:110
  18.5 22.3 %collective-permute-start.1 = (bf16[1,128,3584]{2,1,0:T(8,128)(2,1)S(1)}, bf16[1,128,3584]{2,1,0:T(8,128)(2,1)}, u32[]{:S(2)}, u32[]{:S(2)}) collective-permute-start(bf16[1,128,3584]{2,1,0:T(8,128)(2,1)S(1)} %copy-done.13), channel_id=1, source_target_pairs={{0,112},{16,0},{32,16},{48,32},{64,48},{80,64},{96,80},{112,96},{1... | collective-permute-start | bytes 2752520 | tf_op jit(solution)/shard_map/ppermute | solution.py:13
  21.2 60.7 %collective-permute-start = (bf16[1,128,3584]{2,1,0:T(8,128)(2,1)}, bf16[1,128,3584]{2,1,0:T(8,128)(2,1)}, u32[]{:S(2)}, u32[]{:S(2)}) collective-permute-start(bf16[1,128,3584]{2,1,0:T(8,128)(2,1)} %param.10), channel_id=1, source_target_pairs={{0,16},{16,32},{32,48},{48,64},{64,80},{80,96},{96,112},{112,0},{1... | collective-permute-start | bytes 2752520 | tf_op jit(solution)/shard_map/ppermute | solution.py:13
  21.7 1.8 copy-start.7
  45.0 38.3 %copy-start.4 = (f32[3584]{0:T(1024)S(1)}, f32[3584]{0:T(1024)}, u32[]{:S(2)}) copy-start(f32[3584]{0:T(1024)} %copy-done.3) | copy-start | bytes 43012
  73.8 44.4 %all-to-all-start.2 = ((bf16[16,20,3584]{2,1,0:T(8,128)(2,1)}), bf16[16,20,3584]{2,1,0:T(8,128)(2,1)}, u32[]{:S(2)}, u32[]{:S(2)}) async-start(bf16[16,20,3584]{2,1,0:T(8,128)(2,1)} %reshape.232), calls=%async_computation.2 | async-start | bytes 5505024 | tf_op jit(solution)/shard_map/all_to_all | solution.py:111
  118.2 45.7 %all-to-all-start = ((bf16[16,20,3584]{2,1,0:T(8,128)(2,1)}), bf16[16,20,3584]{2,1,0:T(8,128)(2,1)}, u32[]{:S(2)}, u32[]{:S(2)}) async-start(bf16[16,20,3584]{2,1,0:T(8,128)(2,1)} %reshape.226), calls=%async_computation | async-start | bytes 5505024 | tf_op jit(solution)/shard_map/all_to_all | solution.py:101
  127.6 6.5 %copy-start.2 = (bf16[320,3584]{1,0:T(8,128)(2,1)S(1)}, bf16[320,3584]{1,0:T(8,128)(2,1)}, u32[]{:S(2)}) copy-start(bf16[320,3584]{1,0:T(8,128)(2,1)} %reshape.235) | copy-start | bytes 6881284
  134.1 6.2 %copy-start.14 = (f32[320,1024]{1,0:T(8,128)}, f32[320,1024]{1,0:T(8,128)S(1)}, u32[]{:S(2)}) copy-start(f32[320,1024]{1,0:T(8,128)S(1)} %fusion.14) | copy-start | bytes 3932164
  140.3 1.1 copy-start.16
  163.9 45.7 %all-to-all-start.5 = ((bf16[16,20,3584]{2,1,0:T(8,128)(2,1)}), bf16[16,20,3584]{2,1,0:T(8,128)(2,1)}, u32[]{:S(2)}, u32[]{:S(2)}) async-start(bf16[16,20,3584]{2,1,0:T(8,128)(2,1)} %reshape.238), calls=%async_computation.5 | async-start | bytes 5505024 | tf_op jit(solution)/shard_map/all_to_all | solution.py:118
  173.3 6.5 %copy-start.15 = (f32[320,1024]{1,0:T(8,128)S(1)}, f32[320,1024]{1,0:T(8,128)}, u32[]{:S(2)}) copy-start(f32[320,1024]{1,0:T(8,128)} %copy-done.14) | copy-start | bytes 3932164
  173.3 12.4 %slice-start = ((s8[7340032]{0:T(1024)(128)(4,1)}), s8[4194304]{0:T(1024)(128)(4,1)S(1)}, s32[]{:S(2)}) async-start(s8[7340032]{0:T(1024)(128)(4,1)} %bitcast.158), calls=%async_computation.6 | async-start | bytes 8388608
  179.8 5.9 %slice-start.1 = ((s8[7340032]{0:T(1024)(128)(4,1)}), s8[3145728]{0:T(1024)(128)(4,1)S(1)}, s32[]{:S(2)}) async-start(s8[7340032]{0:T(1024)(128)(4,1)} %bitcast.158), calls=%async_computation.7 | async-start | bytes 6291456
  179.8 5.9 %copy-start.17 = (f32[320,1024]{1,0:T(8,128)S(1)}, f32[320,1024]{1,0:T(8,128)}, u32[]{:S(2)}) copy-start(f32[320,1024]{1,0:T(8,128)} %copy-done.16) | copy-start | bytes 3932164
  209.6 45.7 %all-to-all-start.4 = ((bf16[16,20,3584]{2,1,0:T(8,128)(2,1)}), bf16[16,20,3584]{2,1,0:T(8,128)(2,1)}, u32[]{:S(2)}, u32[]{:S(2)}) async-start(bf16[16,20,3584]{2,1,0:T(8,128)(2,1)} %reshape.236), calls=%async_computation.4 | async-start | bytes 5505024 | tf_op jit(solution)/shard_map/all_to_all | solution.py:117
  255.3 45.7 %all-to-all-start.1 = ((bf16[16,20,3584]{2,1,0:T(8,128)(2,1)}), bf16[16,20,3584]{2,1,0:T(8,128)(2,1)}, u32[]{:S(2)}, u32[]{:S(2)}) async-start(bf16[16,20,3584]{2,1,0:T(8,128)(2,1)} %reshape.228), calls=%async_computation.1 | async-start | bytes 5505024 | tf_op jit(solution)/shard_map/all_to_all | solution.py:103
  264.7 4.2 %copy-start.6 = (s32[128,2]{0,1:T(2,128)S(1)}, s32[128,2]{0,1:T(2,128)}, u32[]{:S(2)}) copy-start(s32[128,2]{0,1:T(2,128)} %copy-done.5) | copy-start | bytes 3076
  268.9 2.9 copy-start.8
  308.2 2.3 copy-start.10
  308.2 2.3 copy-start.12
where the time goes:
time: 315 us; the launch traced here: 313 us
  waiting for transfers between devices  125 us (40%)
  matrix products  70.8 us (22%)
  starting transfers between devices  57.8 us (18%)
  local copies, waits for them, and re-layouts  46.3 us (15%)
  other arithmetic  12.4 us (4%)
    all_to_all x1, waiting for transfers between devices, per_device(): lax.all_to_all(send_n, 'expert', split_axis=0, concat_axis=0, tiled=True)  28.8 us
    all_to_all x1, waiting for transfers between devices, per_device(): lax.all_to_all(expert_forward(rows, wg, wu, wd).reshape(items.shape), 'ex...  24.7 us
    all_to_all x1, waiting for transfers between devices, per_device(): lax.all_to_all(send_c, 'expert', split_axis=0, concat_axis=0, tiled=True)  23.3 us
    ppermute x2, waiting for transfers between devices, from_behind(): return lax.ppermute(value, axis, pairs)  17.4 us
    dot_general x1, matrix products, expert_forward(): jnp.dot(act, wd, preferred_element_type=jnp.float32).astype(jnp.bfloat16)  12.5 us
    all_to_all x1, waiting for transfers between devices, per_device(): lax.all_to_all(unit_part, 'expert', split_axis=0, concat_axis=0, tiled=True)  12.3 us
    all_to_all x1, waiting for transfers between devices, per_device(): lax.all_to_all(extra, 'expert', split_axis=0, concat_axis=0, tiled=True)  11.3 us
    reshape x3, local copies, waits for them, and re-layouts, collect(): flat = returned.reshape(-1, returned.shape[-1])  11 us
  transfers between devices with their start and end apart: 8, of which 7 were waited for; matrix products, arithmetic and copies ran while one was open for 34% of the time, Pallas kernels for 0%

commit v1 on v0

v1 whole, which is shorter than its diff:
```python
import functools

import jax
import jax.numpy as jnp
from jax import lax
from jax.experimental import pallas as pl
from jax.experimental.pallas import tpu as pltpu
from jax.sharding import PartitionSpec as P

MESH = pl.DeviceIdType.MESH
F32, BF16 = jnp.float32, jnp.bfloat16
route_scale = 2.5
epsilon = 1e-06

D, H, T, E = 3584, 1024, 128, 16
MAIN, OVER, PARTS = 16, 4, 4
WIDE = D // PARTS
BLOCK = MAIN * PARTS + OVER * PARTS
ROWS = E * (MAIN + OVER)
HALF = E // 2
HTILE = 256
NONE = -1000.0


def nt(a, b):
    return lax.dot_general(a, b, (((1,), (1,)), ((), ())), preferred_element_type=F32)


def nn(a, b):
    return jnp.dot(a, b, preferred_element_type=F32)


def iota(shape, axis):
    return lax.broadcasted_iota(jnp.int32, shape, axis)


def route(ids):
    lanes = iota((T, T), 1)
    hot = [(lanes == ids[:, k : k + 1]).astype(F32) for k in (0, 1)]
    tri = (iota((T, T), 0) > lanes).astype(BF16)
    before = nn(tri, (hot[0] + hot[1]).astype(BF16))
    packed = jnp.full((T, T), NONE, F32)
    for k in (0, 1):
        slot = jnp.sum(hot[k] * before, axis=1, keepdims=True)
        base = (ids[:, k : k + 1] * MAIN).astype(F32)
        packed = jnp.where(lanes == k, jnp.where(slot < MAIN, base + slot, NONE), packed)
        packed = jnp.where(lanes == 2 + k, jnp.where(slot < MAIN, NONE, base + slot - MAIN), packed)
    return packed


def picks(rows, places, base, shift):
    at = (iota((T, T), 0) + base).astype(F32)
    return sum((at == rows[p : p + 1, :] + shift).astype(F32) for p in places).astype(BF16)


def gates(logits, ids):
    lanes = iota((T, E), 1)
    score = [
        jax.nn.sigmoid(jnp.sum(jnp.where(lanes == ids[:, k : k + 1], logits, 0.0), axis=1, keepdims=True))
        for k in (0, 1)
    ]
    total = score[0] + score[1]
    return score, total, [route_scale * s / total for s in score]


def spread(places, values, shift):
    at = iota((T, E * MAIN), 1).astype(F32)
    return sum(jnp.where(at == p + shift, v, 0.0) for p, v in zip(places, values)).astype(BF16)


def kernel(
    fwd_hbm, saved_hbm, cot_hbm, idf_hbm, idb_hbm, gain_hbm, router_hbm, wg_hbm, wu_hbm, wd_hbm,
    of_hbm, ob_hbm,
    wg, wu, wd, a1s, a1r, a2s, a2r, a3s, a3r, r1r, r2r, ps, pr,
    xr, cr, saved, normed, arr_f, arr_b, dg, du, scaled, router, gain, idf, idb, colf, colb, gf, gb,
    ssem, rsem, hsem, lsem, osem,
):
    s, e = lax.axis_index("section"), lax.axis_index("expert")
    layers = lax.axis_size("section")
    after, ahead = (s + 1) % layers, (s + layers - 1) % layers
    yhi = e // HALF

    loads = [
        pltpu.make_async_copy(src, dst, lsem.at[i])
        for i, (src, dst) in enumerate(
            [(saved_hbm, saved), (idb_hbm, idb), (gain_hbm, gain), (idf_hbm, idf), (router_hbm, router),
             (wg_hbm, wg), (wu_hbm, wu), (wd_hbm, wd)]
        )
    ]
    for load in loads[:3]:
        load.start()

    barrier = pltpu.get_barrier_semaphore()

    def greet(d, _):
        pl.semaphore_signal(barrier, inc=1, device_id=(s, (e + d) % E), device_id_type=MESH)
        return 0

    lax.fori_loop(1, E, greet, 0)
    for t in (after, ahead):
        pl.semaphore_signal(barrier, inc=1, device_id=(t, e), device_id_type=MESH)
    pl.semaphore_wait(barrier, E + 1)

    hop_f = pltpu.make_async_remote_copy(
        fwd_hbm, arr_f, hsem.at[0], hsem.at[1], device_id=(after, e), device_id_type=MESH)
    hop_b = pltpu.make_async_remote_copy(
        cot_hbm, arr_b, hsem.at[2], hsem.at[3], device_id=(ahead, e), device_id_type=MESH)
    hop_b.start()
    hop_f.start()
    for load in loads[3:]:
        load.start()

    def remote(k, src, dst, p, at):
        return pltpu.make_async_remote_copy(
            src.at[p], dst.at[at], ssem.at[k, p], rsem.at[k, at], device_id=(s, p), device_id_type=MESH)

    def own(k, src, dst):
        return pltpu.make_async_copy(src.at[e], dst.at[e], rsem.at[k, e])

    def send(k, src, dst, first, last):
        def step(d, _):
            remote(k, src, dst, (e + d) % E, e).start()
            return 0

        if first == 0:
            own(k, src, dst).start()
        lax.fori_loop(max(first, 1), last, step, 0)

    def send_half(k, src, dst, half):
        def step(i, _):
            p = half * HALF + (e + i) % HALF
            remote(k, src, dst, p, e).start()
            return 0

        lax.fori_loop(1, HALF, step, 0)

    def arrive(k, src, dst):
        def step(d, _):
            p = (e + d) % E
            remote(k, src, dst, p, p).wait_recv()
            return 0

        lax.fori_loop(1, E, step, 0)
        own(k, src, dst).wait()

    def sent(k, src, dst):
        def step(d, _):
            remote(k, src, dst, (e + d) % E, e).wait_send()
            return 0

        lax.fori_loop(1, E, step, 0)

    def norm(x_ref, out):
        x = x_ref[...].astype(F32)
        inv = lax.rsqrt(jnp.sum(x * x, axis=1, keepdims=True) * (1.0 / D) + epsilon)
        out[...] = (x * inv * gain[...].astype(F32)).astype(BF16)
        return inv

    def pack(x_ref, rows, buf, half):
        base = half * (HALF * MAIN)
        main = picks(rows, (0, 1), base, 0.0)

        def step(q, _):
            got = nn(main, x_ref[:, pl.ds(pl.multiple_of(q * WIDE, 128), WIDE)]).astype(BF16)
            buf[pl.ds(half * HALF, HALF), pl.ds(pl.multiple_of(q * MAIN, MAIN), MAIN), :] = got.reshape(HALF, MAIN, WIDE)
            return 0

        lax.fori_loop(0, PARTS, step, 0)
        over = sum(
            nn(picks(rows, (2, 3), base, float(OVER * q)), x_ref[:, q * WIDE : (q + 1) * WIDE])
            for q in range(PARTS)
        )
        buf[pl.ds(half * HALF, HALF), MAIN * PARTS : BLOCK, :] = over.astype(BF16).reshape(HALF, MAIN, WIDE)

    def dispatch(k, x_ref, rows, src, dst):
        for near in (True, False):
            half = yhi if near else 1 - yhi
            pack(x_ref, rows, src, half)
            if near:
                own(k, src, dst).start()
                send_half(k, src, dst, half)
            else:
                send_half(k, src, dst, half)
                remote(k, src, dst, half * HALF + e % HALF, e).start()

    def unpack(buf, out):
        tail = buf[:, MAIN * PARTS : BLOCK, :].reshape(E * MAIN, WIDE)
        row, lane = iota((E * OVER, E * MAIN), 0), iota((E * OVER, E * MAIN), 1)

        def step(q, _):
            columns = pl.ds(pl.multiple_of(q * WIDE, 128), WIDE)
            out[0 : E * MAIN, columns] = buf[:, pl.ds(pl.multiple_of(q * MAIN, MAIN), MAIN), :].reshape(E * MAIN, WIDE)
            pick = (lane == (row // OVER) * MAIN + OVER * q + row % OVER).astype(BF16)
            out[E * MAIN : ROWS, columns] = nn(pick, tail).astype(BF16)
            return 0

        lax.fori_loop(0, PARTS, step, 0)

    def lay(q, buf, value):
        low = value.astype(BF16)
        buf[:, pl.ds(pl.multiple_of(q * MAIN, MAIN), MAIN), :] = low[0 : E * MAIN].reshape(E, MAIN, WIDE)
        row, lane = iota((E * MAIN, E * OVER), 0), iota((E * MAIN, E * OVER), 1)
        here = (lane == (row // MAIN) * OVER + row % OVER) & (row % MAIN // OVER == q)
        return nn(here.astype(BF16), low[E * MAIN : ROWS])

    for load in loads[:3]:
        load.wait()
    inv_b = norm(saved, normed)
    gb[:, 0:1] = inv_b
    packed = route(idb[...])
    colb[...] = packed
    rows_b = jnp.transpose(packed)[0:8, :]
    dispatch(0, normed, rows_b, a1s, a1r)
    loads[4].wait()
    score, total, weight = gates(nn(normed[...], router[...]), idb[...])
    gb[:, 1:2], gb[:, 2:3], gb[:, 3:4] = score[0], score[1], total
    gb[:, 4:5], gb[:, 5:6] = weight[0], weight[1]

    hop_b.wait_recv()
    dispatch(1, arr_b, rows_b, a2s, a2r)

    loads[3].wait()
    hop_f.wait_recv()
    norm(arr_f, normed)
    packed = route(idf[...])
    colf[...] = packed
    dispatch(2, normed, jnp.transpose(packed)[0:8, :], a3s, a3r)
    score, total, weight = gates(nn(normed[...], router[...]), idf[...])
    gf[:, 0:1], gf[:, 1:2] = weight[0], weight[1]

    for load in loads[5:]:
        load.wait()
    arrive(0, a1s, a1r)
    unpack(a1r, xr)
    arrive(1, a2s, a2r)
    unpack(a2r, cr)

    def hidden(n, prod):
        columns = pl.ds(pl.multiple_of(n * HTILE, HTILE), HTILE)
        gate, up = nn(xr[...], wg[:, columns]), nn(xr[...], wu[:, columns])
        grad = nt(cr[...], wd[columns, :])
        sig = jax.nn.sigmoid(gate)
        act = (gate * sig * up).astype(BF16).astype(F32)
        dg[:, columns] = (grad * up * sig * (1.0 + gate * (1.0 - sig))).astype(BF16)
        du[:, columns] = (grad * gate * sig).astype(BF16)
        return prod + jnp.sum(act * grad, axis=1, keepdims=True)

    prod = lax.fori_loop(0, H // HTILE, hidden, jnp.zeros((ROWS, 1), F32))
    prod = jnp.broadcast_to(prod, (ROWS, T)).astype(BF16)
    ps[:, 0:MAIN, :] = prod[0 : E * MAIN].reshape(E, MAIN, T)
    row, lane = iota((E * MAIN, E * OVER), 0), iota((E * MAIN, E * OVER), 1)
    here = (lane == (row // MAIN) * OVER + row % OVER).astype(BF16)
    ps[:, MAIN : 2 * MAIN, :] = nn(here, prod[E * MAIN : ROWS]).astype(BF16).reshape(E, MAIN, T)
    send(3, ps, pr, 0, E)

    sent(0, a1s, a1r)

    def unit(q, over):
        rows = pl.ds(pl.multiple_of(q * WIDE, 128), WIDE)
        return over + lay(q, a1s, nt(dg[...], wg[rows, :]) + nt(du[...], wu[rows, :]))

    over = lax.fori_loop(0, PARTS, unit, jnp.zeros((E * MAIN, WIDE), F32))
    a1s[:, MAIN * PARTS : BLOCK, :] = over.astype(BF16).reshape(E, MAIN, WIDE)
    send(4, a1s, r1r, 0, E)

    arrive(2, a3s, a3r)
    unpack(a3r, xr)

    def hidden_f(n, _):
        columns = pl.ds(pl.multiple_of(n * HTILE, HTILE), HTILE)
        gate, up = nn(xr[...], wg[:, columns]), nn(xr[...], wu[:, columns])
        dg[:, columns] = (gate * jax.nn.sigmoid(gate) * up).astype(BF16)
        return 0

    lax.fori_loop(0, H // HTILE, hidden_f, 0)
    sent(1, a2s, a2r)

    def down(q, over):
        columns = pl.ds(pl.multiple_of(q * WIDE, 128), WIDE)
        return over + lay(q, a2s, nn(dg[...], wd[:, columns]))

    over = lax.fori_loop(0, PARTS, down, jnp.zeros((E * MAIN, WIDE), F32))
    a2s[:, MAIN * PARTS : BLOCK, :] = over.astype(BF16).reshape(E, MAIN, WIDE)
    send(5, a2s, r2r, 0, E)

    arrive(3, ps, pr)
    arrive(4, a1s, r1r)
    places = [colb[:, p : p + 1] for p in range(4)]
    score, total = [gb[:, 1:2], gb[:, 2:3]], gb[:, 3:4]
    weight = [gb[:, 4:5], gb[:, 5:6]]
    inv = gb[:, 0:1]
    one = jnp.ones((T, 1), F32)
    product = []
    for k in (0, 1):
        got = nn(spread([places[k]], [one], 0.0), pr[:, 0:MAIN, :].reshape(E * MAIN, T))
        got += nn(spread([places[2 + k]], [one], 0.0), pr[:, MAIN : 2 * MAIN, :].reshape(E * MAIN, T))
        product.append(got[:, 0:1])
    mixed = (product[0] * weight[0] + product[1] * weight[1]) * (1.0 / route_scale)
    lanes = iota((T, E), 1)
    dlogits = jnp.zeros((T, E), F32)
    for k in (0, 1):
        dlogit = route_scale / total * (product[k] - mixed) * score[k] * (1.0 - score[k])
        dlogits += jnp.where(lanes == idb[:, k : k + 1], dlogit, 0.0)
    dlogits = dlogits.astype(BF16)
    main_w = spread(places[0:2], weight, 0.0)

    def grad_in(q, dot):
        columns = pl.ds(pl.multiple_of(q * WIDE, 128), WIDE)
        over_w = spread(places[2:4], weight, (OVER * q).astype(F32))
        got = nn(main_w, r1r[:, pl.ds(pl.multiple_of(q * MAIN, MAIN), MAIN), :].reshape(E * MAIN, WIDE))
        got += nn(over_w, r1r[:, MAIN * PARTS : BLOCK, :].reshape(E * MAIN, WIDE))
        got += nt(dlogits, router[pl.ds(pl.multiple_of(q * WIDE, 128), WIDE), :])
        got *= gain[:, columns].astype(F32)
        scaled[:, columns] = got
        return dot + jnp.sum(got * saved[:, columns].astype(F32), axis=1, keepdims=True)

    dot = lax.fori_loop(0, PARTS, grad_in, jnp.zeros((T, 1), F32)) * (1.0 / D)
    back = inv * inv * inv * dot

    def finish_b(q, _):
        columns = pl.ds(pl.multiple_of(q * WIDE, 128), WIDE)
        dx = inv * scaled[:, columns] - saved[:, columns].astype(F32) * back
        saved[:, columns] = (arr_b[:, columns].astype(F32) + dx).astype(BF16)
        return 0

    lax.fori_loop(0, PARTS, finish_b, 0)
    out_b = pltpu.make_async_copy(saved, ob_hbm, osem.at[0])
    out_b.start()

    places_f = [colf[:, p : p + 1] for p in range(4)]
    weight_f = [gf[:, 0:1], gf[:, 1:2]]
    main_f = spread(places_f[0:2], weight_f, 0.0)
    arrive(5, a2s, r2r)

    def finish_f(q, _):
        columns = pl.ds(pl.multiple_of(q * WIDE, 128), WIDE)
        over_w = spread(places_f[2:4], weight_f, (OVER * q).astype(F32))
        got = nn(main_f, r2r[:, pl.ds(pl.multiple_of(q * MAIN, MAIN), MAIN), :].reshape(E * MAIN, WIDE))
        got += nn(over_w, r2r[:, MAIN * PARTS : BLOCK, :].reshape(E * MAIN, WIDE))
        normed[:, columns] = (arr_f[:, columns].astype(F32) + got).astype(BF16)
        return 0

    lax.fori_loop(0, PARTS, finish_f, 0)
    out_f = pltpu.make_async_copy(normed, of_hbm, osem.at[1])
    out_f.start()
    hop_f.wait_send()
    hop_b.wait_send()
    sent(2, a3s, a3r)
    sent(3, ps, pr)
    sent(4, a1s, r1r)
    sent(5, a2s, r2r)
    out_b.wait()
    out_f.wait()


def per_device(fwd_acts, bwd_saved, bwd_cot, fwd_ids, bwd_ids, norm_gain, router, w_gate, w_up, w_down):
    def vm(*shape, dtype=BF16):
        return pltpu.VMEM(shape, dtype)

    block = (E, BLOCK, WIDE)
    scratch = [
        vm(D, H), vm(D, H), vm(H, D),
        *[vm(*block) for _ in range(8)],
        vm(E, 2 * MAIN, T), vm(E, 2 * MAIN, T),
        vm(ROWS, D), vm(ROWS, D),
        vm(T, D), vm(T, D), vm(T, D), vm(T, D),
        vm(ROWS, H), vm(ROWS, H),
        vm(T, D, dtype=F32),
        vm(D, E), vm(1, D),
        vm(T, 2, dtype=jnp.int32), vm(T, 2, dtype=jnp.int32),
        vm(T, T, dtype=F32), vm(T, T, dtype=F32), vm(T, T, dtype=F32), vm(T, T, dtype=F32),
        pltpu.SemaphoreType.DMA((6, E)), pltpu.SemaphoreType.DMA((6, E)),
        pltpu.SemaphoreType.DMA((4,)), pltpu.SemaphoreType.DMA((8,)), pltpu.SemaphoreType.DMA((2,)),
    ]
    out = jax.ShapeDtypeStruct((T, D), BF16)
    fwd_out, bwd_grad = pl.pallas_call(
        kernel,
        out_shape=(out, out),
        in_specs=[pl.BlockSpec(memory_space=pl.ANY)] * 10,
        out_specs=(pl.BlockSpec(memory_space=pl.ANY),) * 2,
        scratch_shapes=scratch,
        name="layer",
        compiler_params=pltpu.CompilerParams(
            collective_id=0, has_side_effects=True, vmem_limit_bytes=62 * 1024 * 1024
        ),
        cost_estimate=pl.CostEstimate(flops=8 * 2 * ROWS * D * H, bytes_accessed=30_000_000, transcendentals=0),
    )(
        fwd_acts[0], bwd_saved[0], bwd_cot[0], fwd_ids[0], bwd_ids[0], norm_gain, router[0],
        w_gate[0, 0], w_up[0, 0], w_down[0, 0],
    )
    return fwd_out[None], bwd_grad[None]


def solution(mesh):
    rows = P("section", "expert", None)
    return jax.shard_map(
        per_device,
        mesh=mesh,
        in_specs=(
            rows, rows, rows, rows, rows, P("section", None), P("section", None, None),
            P("section", "expert", None, None), P("section", "expert", None, None), P("section", "expert", None, None),
        ),
        out_specs=(rows, rows),
        check_vma=False,
    )
```

time: 315 us -> 187 us (0.59)
  the two profiles are of different devices: /device:TPU:1 before, /device:TPU:113 now
where the time goes in v1:
time: 187 us; the launch traced here: 186 us
  Pallas kernels  176 us (94%)
  local copies, waits for them, and re-layouts  9.27 us (5%)
    pallas_call x1, Pallas kernels, per_device(): pl.pallas_call(kernel, out_shape=(out, out), in_specs=[pl.BlockSpec(memor...  176 us
    unnamed x5, local copies, waits for them, and re-layouts  9.27 us

profile of v1, /device:TPU:113, one launch (start us, length us, event | category | flops | bytes accessed | tf_op | source)
XLA Modules:
  0.0 186.4 jit_solution(6371775274032257946)
XLA Ops:
  0.6 1.4 copy.12
  2.0 1.4 copy.13
  3.4 2.1 %copy.14 = bf16[1,3584,16]{2,1,0:T(8,128)(2,1)} copy(bf16[1,3584,16]{1,2,0:T(8,128)(2,1)} %param.16) | data formatting | bytes 229376 | tf_op args[6]
  5.6 176.5 %layer.1 = (bf16[128,3584]{1,0:T(8,128)(2,1)}, bf16[128,3584]{1,0:T(8,128)(2,1)}) custom-call(bf16[128,3584]{1,0:T(8,128)(2,1)} %bitcast.19, bf16[128,3584]{1,0:T(8,128)(2,1)} %bitcast.20, bf16[128,3584]{1,0:T(8,128)(2,1)} %bitcast.21, s32[128,2]{1,0:T(8,128)} %bitcast.14, s32[128,2]{1,0:T(8,128)} %bitcast.15, bf16[1,3584]{1,0:T(2,128)(2,1)} %gain_hbm.1, ...), custom_call_target="tpu_custom_call" | custom-call | flops 18790481920 | bytes 30000000 | tf_op jit(solution)/shard_map/layer/pallas_call | solution.py:376
  182.1 2.2 %copy.17 = bf16[1,128,3584]{2,1,0:T(8,128)(2,1)} copy(bf16[1,128,3584]{2,1,0:T(8,128)(2,1)} %bitcast.12) | data formatting | bytes 1835008
  184.2 2.2 %copy.18 = bf16[1,128,3584]{2,1,0:T(8,128)(2,1)} copy(bf16[1,128,3584]{2,1,0:T(8,128)(2,1)} %bitcast.11) | data formatting | bytes 1835008

commit v2 on v1

v2 whole, which is shorter than its diff:
```python
import functools

import jax
import jax.numpy as jnp
from jax import lax
from jax.experimental import pallas as pl
from jax.experimental.pallas import tpu as pltpu
from jax.sharding import PartitionSpec as P

MESH = pl.DeviceIdType.MESH
F32, BF16 = jnp.float32, jnp.bfloat16
route_scale = 2.5
epsilon = 1e-06

D, H, T, E = 3584, 1024, 128, 16
MAIN, OVER, PARTS = 16, 4, 4
WIDE = D // PARTS
BLOCK = MAIN * PARTS + OVER * PARTS
ROWS = E * (MAIN + OVER)
HALF = E // 2
HTILE = 256
NONE = -1000.0


def nt(a, b):
    return lax.dot_general(a, b, (((1,), (1,)), ((), ())), preferred_element_type=F32)


def nn(a, b):
    return jnp.dot(a, b, preferred_element_type=F32)


def iota(shape, axis):
    return lax.broadcasted_iota(jnp.int32, shape, axis)


def route(ids):
    at = iota((E, T), 0)
    hot = [(at == ids[k : k + 1, :]).astype(F32) for k in (0, 1)]
    tri = (iota((T, T), 0) < iota((T, T), 1)).astype(BF16)
    before = nn((hot[0] + hot[1]).astype(BF16), tri)
    line = iota((8, T), 0)
    rows = jnp.zeros((8, T), F32)
    for k in (0, 1):
        slot = jnp.sum(hot[k] * before, axis=0, keepdims=True)
        named = ids[k : k + 1, :].astype(F32)
        base = named * float(MAIN)
        rows = jnp.where(line == k, jnp.where(slot < MAIN, base + slot, NONE), rows)
        rows = jnp.where(line == 2 + k, jnp.where(slot < MAIN, NONE, base + slot - MAIN), rows)
        rows = jnp.where(line == 4 + k, named, rows)
    return rows


def stand(rows):
    return jnp.transpose(jnp.concatenate([rows, jnp.zeros((T - 8, T), F32)], axis=0))


def picks(rows, places, base, shift):
    at = (iota((T, T), 0) + base).astype(F32)
    return sum((at == rows[p : p + 1, :] + shift).astype(F32) for p in places).astype(BF16)


def gates(logits, columns):
    lanes = iota((T, E), 1).astype(F32)
    score = [
        jax.nn.sigmoid(jnp.sum(jnp.where(lanes == columns[:, 4 + k : 5 + k], logits, 0.0), axis=1, keepdims=True))
        for k in (0, 1)
    ]
    total = score[0] + score[1]
    return score, total, [route_scale * s / total for s in score]


def spread(places, values, shift):
    at = iota((T, E * MAIN), 1).astype(F32)
    return sum(jnp.where(at == p + shift, v, 0.0) for p, v in zip(places, values)).astype(BF16)


def kernel(
    fwd_hbm, saved_hbm, cot_hbm, idf_hbm, idb_hbm, gain_hbm, router_hbm, wg_hbm, wu_hbm, wd_hbm,
    of_hbm, ob_hbm,
    wg, wu, wd, a1s, a1r, a2s, a2r, a3s, a3r, r1r, r2r, ps, pr,
    xr, cr, saved, normed, arr_f, arr_b, dg, du, gates_b, ups_b, scaled, router, gain,
    idf, idb, rowf, rowb, colf, colb, gf, gb,
    ssem, rsem, hsem, lsem, osem,
):
    s, e = lax.axis_index("section"), lax.axis_index("expert")
    layers = lax.axis_size("section")
    after, ahead = (s + 1) % layers, (s + layers - 1) % layers
    yhi, zed, core = e // HALF, e // 2 % 4, e % 2
    near, far = yhi * HALF, (1 - yhi) * HALF

    loads = [
        pltpu.make_async_copy(src, dst, lsem.at[i])
        for i, (src, dst) in enumerate(
            [(saved_hbm, saved), (idb_hbm, idb), (gain_hbm, gain), (idf_hbm, idf),
             (router_hbm, router), (wg_hbm, wg), (wu_hbm, wu), (wd_hbm, wd)]
        )
    ]
    for load in loads[:4]:
        load.start()

    barrier = pltpu.get_barrier_semaphore()

    def greet(d, _):
        pl.semaphore_signal(barrier, inc=1, device_id=(s, (e + d) % E), device_id_type=MESH)
        return 0

    for t in (after, ahead):
        pl.semaphore_signal(barrier, inc=1, device_id=(t, e), device_id_type=MESH)
    lax.fori_loop(1, E, greet, 0)

    def hop(src, dst, i, t):
        return pltpu.make_async_remote_copy(
            src, dst, hsem.at[2 * i], hsem.at[2 * i + 1], device_id=(t, e), device_id_type=MESH)

    hop_f, hop_b = hop(fwd_hbm, arr_f, 0, after), hop(cot_hbm, arr_b, 1, ahead)

    def near_peer(i):
        return near + (zed + i // 2 + 1) % 4 * 2 + (core + i + 1) % 2

    def far_peer(i):
        return far + (zed + 2 + i // 2 * 3) % 4 * 2 + (core + i) % 2

    def near_from(i):
        return near + (zed + 3 - i // 2) % 4 * 2 + (core + i + 1) % 2

    def far_from(i):
        return far + (zed + 2 + i // 2) % 4 * 2 + (core + i) % 2

    def remote(k, src, dst, p, at):
        return pltpu.make_async_remote_copy(
            src.at[p], dst.at[at], ssem.at[k, p], rsem.at[k, at], device_id=(s, p), device_id_type=MESH)

    def own(k, src, dst):
        return pltpu.make_async_copy(src.at[e], dst.at[e], rsem.at[k, e])

    def each(count, act):
        def step(i, _):
            act(i)
            return 0

        lax.fori_loop(0, count, step, 0)

    def send_far(k, src, dst):
        each(HALF, lambda i: remote(k, src, dst, far_peer(i), e).start())

    def send_near(k, src, dst):
        each(HALF - 1, lambda i: remote(k, src, dst, near_peer(i), e).start())
        own(k, src, dst).start()

    def send(k, src, dst):
        send_far(k, src, dst)
        send_near(k, src, dst)

    def arrive(k, src, dst):
        def wait(p):
            remote(k, src, dst, p, p).wait_recv()

        each(HALF - 1, lambda i: wait(near_from(i)))
        each(HALF, lambda i: wait(far_from(i)))
        own(k, src, dst).wait()

    def sent(k, src, dst):
        def wait(p):
            remote(k, src, dst, p, e).wait_send()

        each(HALF - 1, lambda i: wait(near_peer(i)))
        each(HALF, lambda i: wait(far_peer(i)))

    def norm(x_ref, by, out):
        x = x_ref[...].astype(F32)
        inv = lax.rsqrt(jnp.sum(x * x, axis=1, keepdims=True) * (1.0 / D) + epsilon)
        out[...] = (x * inv * by[...].astype(F32)).astype(BF16)
        return inv

    def pack(x_ref, rows, buf, first):
        base = first * MAIN
        main = picks(rows, (0, 1), base, 0.0)

        def step(q, _):
            got = nn(main, x_ref[:, pl.ds(pl.multiple_of(q * WIDE, 128), WIDE)]).astype(BF16)
            buf[pl.ds(first, HALF), pl.ds(pl.multiple_of(q * MAIN, MAIN), MAIN), :] = got.reshape(HALF, MAIN, WIDE)
            return 0

        lax.fori_loop(0, PARTS, step, 0)
        over = sum(
            nn(picks(rows, (2, 3), base, float(OVER * q)), x_ref[:, q * WIDE : (q + 1) * WIDE])
            for q in range(PARTS)
        )
        buf[pl.ds(first, HALF), MAIN * PARTS : BLOCK, :] = over.astype(BF16).reshape(HALF, MAIN, WIDE)

    def dispatch(k, x_ref, rows, src, dst):
        pack(x_ref, rows, src, far)
        send_far(k, src, dst)
        pack(x_ref, rows, src, near)
        send_near(k, src, dst)

    def unpack(buf, out):
        tail = buf[:, MAIN * PARTS : BLOCK, :].reshape(E * MAIN, WIDE)
        row, lane = iota((E * OVER, E * MAIN), 0), iota((E * OVER, E * MAIN), 1)

        def step(q, _):
            columns = pl.ds(pl.multiple_of(q * WIDE, 128), WIDE)
            out[0 : E * MAIN, columns] = buf[:, pl.ds(pl.multiple_of(q * MAIN, MAIN), MAIN), :].reshape(E * MAIN, WIDE)
            pick = (lane == (row // OVER) * MAIN + OVER * q + row % OVER).astype(BF16)
            out[E * MAIN : ROWS, columns] = nn(pick, tail).astype(BF16)
            return 0

        lax.fori_loop(0, PARTS, step, 0)

    def lay(q, buf, value):
        low = value.astype(BF16)
        buf[:, pl.ds(pl.multiple_of(q * MAIN, MAIN), MAIN), :] = low[0 : E * MAIN].reshape(E, MAIN, WIDE)
        row, lane = iota((E * MAIN, E * OVER), 0), iota((E * MAIN, E * OVER), 1)
        here = (lane == (row // MAIN) * OVER + row % OVER) & (row % MAIN // OVER == q)
        return nn(here.astype(BF16), low[E * MAIN : ROWS])

    scope = jax.named_scope
    with scope("start"):
        loads[1].wait()
        rowb[...] = route(idb[...])
        loads[3].wait()
        rowf[...] = route(idf[...])
        loads[0].wait()
        loads[2].wait()
        gb[:, 0:1] = norm(saved, gain, normed)
    with scope("barrier"):
        pl.semaphore_wait(barrier, E + 1)
    with scope("rows_b_out"):
        for copy in (hop_b, hop_f, *loads[4:]):
            copy.start()
        dispatch(0, normed, rowb, a1s, a1r)
    with scope("gating_b"):
        colb[...] = stand(rowb[...])
        loads[4].wait()
        score, total, weight = gates(nt(normed[...], router[...]), colb)
        gb[:, 1:2], gb[:, 2:3], gb[:, 3:4] = score[0], score[1], total
        gb[:, 4:5], gb[:, 5:6] = weight[0], weight[1]
    with scope("wait_hop_b"):
        hop_b.wait_recv()
    with scope("cot_near_out"):
        dispatch(1, arr_b, rowb, a2s, a2r)
    with scope("wait_hop_f"):
        hop_f.wait_recv()
    with scope("fwd_near_pack"):
        norm(arr_f, gain, normed)
        dispatch(2, normed, rowf, a3s, a3r)
        colf[...] = stand(rowf[...])
        score, total, weight = gates(nt(normed[...], router[...]), colf)
        gf[:, 0:1], gf[:, 1:2] = weight[0], weight[1]
    with scope("wait_rows_b"):
        for load in loads[5:]:
            load.wait()
        arrive(0, a1s, a1r)
    with scope("gate_up_b"):
        unpack(a1r, xr)

        def gate_up(n, _):
            columns = pl.ds(pl.multiple_of(n * HTILE, HTILE), HTILE)
            gates_b[:, columns] = nn(xr[...], wg[:, columns])
            ups_b[:, columns] = nn(xr[...], wu[:, columns])
            return 0

        lax.fori_loop(0, H // HTILE, gate_up, 0)
    with scope("wait_cot"):
        arrive(1, a2s, a2r)

    def hidden(n, prod):
        columns = pl.ds(pl.multiple_of(n * HTILE, HTILE), HTILE)
        gate, up = gates_b[:, columns], ups_b[:, columns]
        grad = nt(cr[...], wd[columns, :])
        sig = jax.nn.sigmoid(gate)
        act = (gate * sig * up).astype(BF16).astype(F32)
        dg[:, columns] = (grad * up * sig * (1.0 + gate * (1.0 - sig))).astype(BF16)
        du[:, columns] = (grad * gate * sig).astype(BF16)
        return prod + jnp.sum(act * grad, axis=1, keepdims=True)

    with scope("hidden_b"):
        unpack(a2r, cr)
        prod = lax.fori_loop(0, H // HTILE, hidden, jnp.zeros((ROWS, 1), F32))
    prod = jnp.broadcast_to(prod, (ROWS, T)).astype(BF16)
    ps[:, 0:MAIN, :] = prod[0 : E * MAIN].reshape(E, MAIN, T)
    row, lane = iota((E * MAIN, E * OVER), 0), iota((E * MAIN, E * OVER), 1)
    here = (lane == (row // MAIN) * OVER + row % OVER).astype(BF16)
    ps[:, MAIN : 2 * MAIN, :] = nn(here, prod[E * MAIN : ROWS]).astype(BF16).reshape(E, MAIN, T)
    send(3, ps, pr)
    with scope("wait_rows_b_sent"):
        sent(0, a1s, a1r)

    def unit(q, over):
        rows = pl.ds(pl.multiple_of(q * WIDE, 128), WIDE)
        return over + lay(q, a1s, nt(dg[...], wg[rows, :]) + nt(du[...], wu[rows, :]))

    with scope("unit_b"):
        over = lax.fori_loop(0, PARTS, unit, jnp.zeros((E * MAIN, WIDE), F32))
    a1s[:, MAIN * PARTS : BLOCK, :] = over.astype(BF16).reshape(E, MAIN, WIDE)
    send(4, a1s, r1r)

    with scope("wait_rows_f"):
        arrive(2, a3s, a3r)

    def hidden_f(n, _):
        columns = pl.ds(pl.multiple_of(n * HTILE, HTILE), HTILE)
        gate, up = nn(xr[...], wg[:, columns]), nn(xr[...], wu[:, columns])
        dg[:, columns] = (gate * jax.nn.sigmoid(gate) * up).astype(BF16)
        return 0

    with scope("hidden_f"):
        unpack(a3r, xr)
        lax.fori_loop(0, H // HTILE, hidden_f, 0)
    with scope("wait_cot_sent"):
        sent(1, a2s, a2r)

    def down(q, over):
        columns = pl.ds(pl.multiple_of(q * WIDE, 128), WIDE)
        return over + lay(q, a2s, nn(dg[...], wd[:, columns]))

    with scope("down_f"):
        over = lax.fori_loop(0, PARTS, down, jnp.zeros((E * MAIN, WIDE), F32))
    a2s[:, MAIN * PARTS : BLOCK, :] = over.astype(BF16).reshape(E, MAIN, WIDE)
    send(5, a2s, r2r)

    with scope("wait_unit"):
        arrive(3, ps, pr)
        arrive(4, a1s, r1r)
    places = [colb[:, p : p + 1] for p in range(4)]
    score, total = [gb[:, 1:2], gb[:, 2:3]], gb[:, 3:4]
    weight = [gb[:, 4:5], gb[:, 5:6]]
    inv = gb[:, 0:1]
    one = jnp.ones((T, 1), F32)
    product = []
    for k in (0, 1):
        got = nn(spread([places[k]], [one], 0.0), pr[:, 0:MAIN, :].reshape(E * MAIN, T))
        got += nn(spread([places[2 + k]], [one], 0.0), pr[:, MAIN : 2 * MAIN, :].reshape(E * MAIN, T))
        product.append(got[:, 0:1])
    mixed = (product[0] * weight[0] + product[1] * weight[1]) * (1.0 / route_scale)
    lanes = iota((T, E), 1).astype(F32)
    dlogits = jnp.zeros((T, E), F32)
    for k in (0, 1):
        dlogit = route_scale / total * (product[k] - mixed) * score[k] * (1.0 - score[k])
        dlogits += jnp.where(lanes == colb[:, 4 + k : 5 + k], dlogit, 0.0)
    dlogits = dlogits.astype(BF16)
    main_w = spread(places[0:2], weight, 0.0)

    def grad_in(q, dot):
        columns = pl.ds(pl.multiple_of(q * WIDE, 128), WIDE)
        over_w = spread(places[2:4], weight, (OVER * q).astype(F32))
        got = nn(main_w, r1r[:, pl.ds(pl.multiple_of(q * MAIN, MAIN), MAIN), :].reshape(E * MAIN, WIDE))
        got += nn(over_w, r1r[:, MAIN * PARTS : BLOCK, :].reshape(E * MAIN, WIDE))
        got += nn(dlogits, router[:, columns])
        got *= gain[:, columns].astype(F32)
        scaled[:, columns] = got
        return dot + jnp.sum(got * saved[:, columns].astype(F32), axis=1, keepdims=True)

    with scope("finish_b"):
        dot = lax.fori_loop(0, PARTS, grad_in, jnp.zeros((T, 1), F32)) * (1.0 / D)
    back = inv * inv * inv * dot

    def finish_b(q, _):
        columns = pl.ds(pl.multiple_of(q * WIDE, 128), WIDE)
        dx = inv * scaled[:, columns] - saved[:, columns].astype(F32) * back
        saved[:, columns] = (arr_b[:, columns].astype(F32) + dx).astype(BF16)
        return 0

    with scope("finish_b2"):
        lax.fori_loop(0, PARTS, finish_b, 0)
    out_b = pltpu.make_async_copy(saved, ob_hbm, osem.at[0])
    out_b.start()

    places_f = [colf[:, p : p + 1] for p in range(4)]
    weight_f = [gf[:, 0:1], gf[:, 1:2]]
    main_f = spread(places_f[0:2], weight_f, 0.0)
    with scope("wait_out_f"):
        arrive(5, a2s, r2r)

    def finish_f(q, _):
        columns = pl.ds(pl.multiple_of(q * WIDE, 128), WIDE)
        over_w = spread(places_f[2:4], weight_f, (OVER * q).astype(F32))
        got = nn(main_f, r2r[:, pl.ds(pl.multiple_of(q * MAIN, MAIN), MAIN), :].reshape(E * MAIN, WIDE))
        got += nn(over_w, r2r[:, MAIN * PARTS : BLOCK, :].reshape(E * MAIN, WIDE))
        normed[:, columns] = (arr_f[:, columns].astype(F32) + got).astype(BF16)
        return 0

    with scope("finish_f"):
        lax.fori_loop(0, PARTS, finish_f, 0)
    out_f = pltpu.make_async_copy(normed, of_hbm, osem.at[1])
    out_f.start()
    with scope("drain"):
        for copy in (hop_b, hop_f):
            copy.wait_send()
        sent(2, a3s, a3r)
        sent(3, ps, pr)
        sent(4, a1s, r1r)
        sent(5, a2s, r2r)
        out_b.wait()
        out_f.wait()


def leave(f_ref, b_ref, of_ref, ob_ref):
    of_ref[...] = f_ref[...]
    ob_ref[...] = b_ref[...]


def per_device(fwd_acts, bwd_saved, bwd_cot, fwd_ids, bwd_ids, norm_gain, router, w_gate, w_up, w_down):
    def vm(*shape, dtype=BF16):
        return pltpu.VMEM(shape, dtype)

    block = (E, BLOCK, WIDE)
    scratch = [
        vm(D, H), vm(D, H), vm(H, D),
        *[vm(*block) for _ in range(8)],
        vm(E, 2 * MAIN, T), vm(E, 2 * MAIN, T),
        vm(ROWS, D), vm(ROWS, D),
        *[vm(T, D) for _ in range(4)],
        vm(ROWS, H), vm(ROWS, H), vm(ROWS, H, dtype=F32), vm(ROWS, H, dtype=F32),
        vm(T, D, dtype=F32),
        vm(E, D), vm(1, D),
        vm(2, T, dtype=jnp.int32), vm(2, T, dtype=jnp.int32),
        *[vm(8, T, dtype=F32) for _ in range(2)],
        *[vm(T, T, dtype=F32) for _ in range(4)],
        pltpu.SemaphoreType.DMA((6, E)), pltpu.SemaphoreType.DMA((6, E)),
        pltpu.SemaphoreType.DMA((4,)), pltpu.SemaphoreType.DMA((8,)), pltpu.SemaphoreType.DMA((2,)),
    ]
    out = jax.ShapeDtypeStruct((T, D), BF16)
    fwd_out, bwd_grad = pl.pallas_call(
        kernel,
        out_shape=(out, out),
        in_specs=[pl.BlockSpec(memory_space=pl.ANY)] * 10,
        out_specs=(pl.BlockSpec(memory_space=pl.ANY),) * 2,
        scratch_shapes=scratch,
        name="layer",
        compiler_params=pltpu.CompilerParams(
            collective_id=0, has_side_effects=True, vmem_limit_bytes=62 * 1024 * 1024
        ),
        cost_estimate=pl.CostEstimate(flops=8 * 2 * ROWS * D * H, bytes_accessed=30_000_000, transcendentals=0),
    )(
        fwd_acts[0], bwd_saved[0], bwd_cot[0], fwd_ids[0].T, bwd_ids[0].T, norm_gain, router[0].T,
        w_gate[0, 0], w_up[0, 0], w_down[0, 0],
    )
    part = pl.BlockSpec((T // 4, D), lambda i: (i, 0))
    fwd_out, bwd_grad = pl.pallas_call(
        leave,
        out_shape=(out, out),
        grid=(4,),
        in_specs=[part, part],
        out_specs=(part, part),
        name="leave",
        cost_estimate=pl.CostEstimate(flops=0, bytes_accessed=4 * 2 * T * D, transcendentals=0),
    )(fwd_out, bwd_grad)
    return fwd_out[None], bwd_grad[None]


def solution(mesh):
    rows = P("section", "expert", None)
    return jax.shard_map(
        per_device,
        mesh=mesh,
        in_specs=(
            rows, rows, rows, rows, rows, P("section", None), P("section", None, None),
            P("section", "expert", None, None), P("section", "expert", None, None), P("section", "expert", None, None),
        ),
        out_specs=(rows, rows),
        check_vma=False,
    )
```

time: 187 us -> 167 us (0.89)
  the two profiles are of different devices: /device:TPU:113 before, /device:TPU:1 now
where the time goes in v2:
time: 167 us
  Pallas kernels  167 us (100%)
    pallas_call x1, Pallas kernels, per_device(): pl.pallas_call(kernel, out_shape=(out, out), in_specs=[pl.BlockSpec(memor...  163 us
    pallas_call x1, Pallas kernels, per_device(): pl.pallas_call(leave, out_shape=(out, out), grid=(4,), in_specs=[part, pa...  3.74 us

profile of v2, /device:TPU:1, one launch (start us, length us, event | category | flops | bytes accessed | tf_op | source)
XLA Modules:
  0.0 167.3 jit_solution(16120415769088388266)
XLA Ops:
  0.6 162.9 %layer.1 = (bf16[128,3584]{1,0:T(8,128)(2,1)}, bf16[128,3584]{1,0:T(8,128)(2,1)}) custom-call(bf16[128,3584]{1,0:T(8,128)(2,1)} %bitcast.20, bf16[128,3584]{1,0:T(8,128)(2,1)} %bitcast.21, bf16[128,3584]{1,0:T(8,128)(2,1)} %bitcast.22, s32[2,128]{1,0:T(2,128)} %bitcast.26, s32[2,128]{1,0:T(2,128)} %bitcast.27, bf16[1,3584]{1,0:T(2,128)(2,1)} %gain_hbm.1, ...), custom_call_target="tpu_custom_call" | custom-call | flops 18790481920 | bytes 30000000 | tf_op jit(solution)/shard_map/layer/pallas_call | solution.py:425
  163.5 3.7 %leave.1 = (bf16[128,3584]{1,0:T(8,128)(2,1)}, bf16[128,3584]{1,0:T(8,128)(2,1)}) custom-call(bf16[128,3584]{1,0:T(8,128)(2,1)} %get-tuple-element.6.f_ref, bf16[128,3584]{1,0:T(8,128)(2,1)} %get-tuple-element.7.b_ref), custom_call_target="tpu_custom_call" | custom-call | bytes 3670016 | tf_op jit(solution)/shard_map/leave/pallas_call | solution.py:441

commit v3 on v2

--- a/solution.py
+++ b/solution.py
@@ -20,6 +20,8 @@
 HALF = E // 2
 HTILE = 256
 NONE = -1000.0
+XS = 4
+QUARTER = T // XS
 
 
 def nt(a, b):
@@ -81,7 +83,7 @@
     wg, wu, wd, a1s, a1r, a2s, a2r, a3s, a3r, r1r, r2r, ps, pr,
     xr, cr, saved, normed, arr_f, arr_b, dg, du, gates_b, ups_b, scaled, router, gain,
     idf, idb, rowf, rowb, colf, colb, gf, gb,
-    ssem, rsem, hsem, lsem, osem,
+    via, ssem, rsem, hsend, hrecv, vsend, vrecv, lsem, osem,
 ):
     s, e = lax.axis_index("section"), lax.axis_index("expert")
     layers = lax.axis_size("section")
@@ -105,15 +107,67 @@
         pl.semaphore_signal(barrier, inc=1, device_id=(s, (e + d) % E), device_id_type=MESH)
         return 0
 
-    for t in (after, ahead):
-        pl.semaphore_signal(barrier, inc=1, device_id=(t, e), device_id_type=MESH)
+    def greet_section(d, _):
+        pl.semaphore_signal(barrier, inc=1, device_id=((s + d) % layers, e), device_id_type=MESH)
+        return 0
+
+    lax.fori_loop(1, layers, greet_section, 0)
     lax.fori_loop(1, E, greet, 0)
 
-    def hop(src, dst, i, t):
+    across, band = s % XS, s // XS
+    blocks = ((fwd_hbm, arr_f), (cot_hbm, arr_b))
+    ways = ((0, 3, 2, 1), (3, 0, 1, 2))
+    towards = (after, ahead)
+    at_end = (across == XS - 1, across == 0)
+
+    def quarter(n, j):
+        rows = pl.ds(j * QUARTER, QUARTER)
         return pltpu.make_async_remote_copy(
-            src, dst, hsem.at[2 * i], hsem.at[2 * i + 1], device_id=(t, e), device_id_type=MESH)
-
-    hop_f, hop_b = hop(fwd_hbm, arr_f, 0, after), hop(cot_hbm, arr_b, 1, ahead)
+            blocks[n][0].at[rows], blocks[n][1].at[rows], hsend.at[n, j], hrecv.at[n, j],
+            device_id=(towards[n], e), device_id_type=MESH)
+
+    def detour(n, j):
+        return pltpu.make_async_remote_copy(
+            blocks[n][0].at[pl.ds(j * QUARTER, QUARTER)], via.at[n], hsend.at[n, j], vrecv.at[n],
+            device_id=((1 - band) * XS + ways[n][j], e), device_id_type=MESH)
+
+    def onward(n, j):
+        return pltpu.make_async_remote_copy(
+            via.at[n], blocks[n][1].at[pl.ds(j * QUARTER, QUARTER)], vsend.at[n], hrecv.at[n, j],
+            device_id=(band * XS + ways[n][0], e), device_id_type=MESH)
+
+    def hop(n):
+        quarter(n, 0).start()
+        for j in range(1, XS):
+
+            @pl.when(at_end[n])
+            def _():
+                detour(n, j).start()
+
+            @pl.when(jnp.logical_not(at_end[n]))
+            def _():
+                quarter(n, j).start()
+
+    def relay(n):
+        for j in range(1, XS):
+
+            @pl.when(across == ways[n][j])
+            def _():
+                detour(n, j).wait_recv()
+                onward(n, j).start()
+
+    def hop_arrive(n):
+        for j in range(XS):
+            quarter(n, j).wait_recv()
+
+    def hop_sent(n):
+        for j in range(XS):
+            quarter(n, j).wait_send()
+        for j in range(1, XS):
+
+            @pl.when(across == ways[n][j])
+            def _():
+                onward(n, j).wait_send()
 
     def near_peer(i):
         return near + (zed + i // 2 + 1) % 4 * 2 + (core + i + 1) % 2
@@ -225,10 +279,12 @@
         loads[2].wait()
         gb[:, 0:1] = norm(saved, gain, normed)
     with scope("barrier"):
-        pl.semaphore_wait(barrier, E + 1)
+        pl.semaphore_wait(barrier, E - 1 + layers - 1)
     with scope("rows_b_out"):
-        for copy in (hop_b, hop_f, *loads[4:]):
-            copy.start()
+        hop(1)
+        hop(0)
+        for load in loads[4:]:
+            load.start()
         dispatch(0, normed, rowb, a1s, a1r)
     with scope("gating_b"):
         colb[...] = stand(rowb[...])
@@ -236,12 +292,15 @@
         score, total, weight = gates(nt(normed[...], router[...]), colb)
         gb[:, 1:2], gb[:, 2:3], gb[:, 3:4] = score[0], score[1], total
         gb[:, 4:5], gb[:, 5:6] = weight[0], weight[1]
+    with scope("relay"):
+        relay(1)
+        relay(0)
     with scope("wait_hop_b"):
-        hop_b.wait_recv()
+        hop_arrive(1)
     with scope("cot_near_out"):
         dispatch(1, arr_b, rowb, a2s, a2r)
     with scope("wait_hop_f"):
-        hop_f.wait_recv()
+        hop_arrive(0)
     with scope("fwd_near_pack"):
         norm(arr_f, gain, normed)
         dispatch(2, normed, rowf, a3s, a3r)
@@ -386,8 +445,8 @@
     out_f = pltpu.make_async_copy(normed, of_hbm, osem.at[1])
     out_f.start()
     with scope("drain"):
-        for copy in (hop_b, hop_f):
-            copy.wait_send()
+        hop_sent(0)
+        hop_sent(1)
         sent(2, a3s, a3r)
         sent(3, ps, pr)
         sent(4, a1s, r1r)
@@ -396,9 +455,22 @@
         out_f.wait()
 
 
-def leave(f_ref, b_ref, of_ref, ob_ref):
-    of_ref[...] = f_ref[...]
-    ob_ref[...] = b_ref[...]
+def leave(f_hbm, b_hbm, of_hbm, ob_hbm, f_ref, b_ref, in_sem, out_sem):
+    pairs = []
+    for i, (src, mid, dst) in enumerate(((f_hbm, f_ref, of_hbm), (b_hbm, b_ref, ob_hbm))):
+        for j in range(4):
+            part = pl.ds(j * (T // 4), T // 4)
+            pairs.append(
+                (pltpu.make_async_copy(src.at[part], mid.at[part], in_sem.at[i, j]),
+                 pltpu.make_async_copy(mid.at[part], dst.at[part], out_sem.at[i, j]))
+            )
+    for come, _ in pairs:
+        come.start()
+    for come, go in pairs:
+        come.wait()
+        go.start()
+    for _, go in pairs:
+        go.wait()
 
 
 def per_device(fwd_acts, bwd_saved, bwd_cot, fwd_ids, bwd_ids, norm_gain, router, w_gate, w_up, w_down):
@@ -418,8 +490,11 @@
         vm(2, T, dtype=jnp.int32), vm(2, T, dtype=jnp.int32),
         *[vm(8, T, dtype=F32) for _ in range(2)],
         *[vm(T, T, dtype=F32) for _ in range(4)],
+        vm(2, QUARTER, D),
         pltpu.SemaphoreType.DMA((6, E)), pltpu.SemaphoreType.DMA((6, E)),
-        pltpu.SemaphoreType.DMA((4,)), pltpu.SemaphoreType.DMA((8,)), pltpu.SemaphoreType.DMA((2,)),
+        pltpu.SemaphoreType.DMA((2, XS)), pltpu.SemaphoreType.DMA((2, XS)),
+        pltpu.SemaphoreType.DMA((2,)), pltpu.SemaphoreType.DMA((2,)),
+        pltpu.SemaphoreType.DMA((8,)), pltpu.SemaphoreType.DMA((2,)),
     ]
     out = jax.ShapeDtypeStruct((T, D), BF16)
     fwd_out, bwd_grad = pl.pallas_call(
@@ -437,13 +512,12 @@
         fwd_acts[0], bwd_saved[0], bwd_cot[0], fwd_ids[0].T, bwd_ids[0].T, norm_gain, router[0].T,
         w_gate[0, 0], w_up[0, 0], w_down[0, 0],
     )
-    part = pl.BlockSpec((T // 4, D), lambda i: (i, 0))
     fwd_out, bwd_grad = pl.pallas_call(
         leave,
         out_shape=(out, out),
-        grid=(4,),
-        in_specs=[part, part],
-        out_specs=(part, part),
+        in_specs=[pl.BlockSpec(memory_space=pl.ANY)] * 2,
+        out_specs=(pl.BlockSpec(memory_space=pl.ANY),) * 2,
+        scratch_shapes=[vm(T, D), vm(T, D), pltpu.SemaphoreType.DMA((2, 4)), pltpu.SemaphoreType.DMA((2, 4))],
         name="leave",
         cost_estimate=pl.CostEstimate(flops=0, bytes_accessed=4 * 2 * T * D, transcendentals=0),
     )(fwd_out, bwd_grad)

time: 167 us -> 157 us (0.940)
  Pallas kernels: 167 us -> 155 us
    pallas_call x1, Pallas kernels: 163 us -> 153 us  [per_device(): pl.pallas_call(kernel, out_shape=(out, out), in_specs=[pl.BlockSpec(memor...]
where the time goes in v3:
time: 157 us; the launch traced here: 156 us
  Pallas kernels  155 us (99%)
    pallas_call x1, Pallas kernels, per_device(): pl.pallas_call(kernel, out_shape=(out, out), in_specs=[pl.BlockSpec(memor...  153 us

profile of v3, /device:TPU:1, one launch (start us, length us, event | category | flops | bytes accessed | tf_op | source)
XLA Modules:
  0.0 155.8 jit_solution(1921361775204275472)
XLA Ops:
  0.6 152.7 %layer.1 = (bf16[128,3584]{1,0:T(8,128)(2,1)}, bf16[128,3584]{1,0:T(8,128)(2,1)}) custom-call(bf16[128,3584]{1,0:T(8,128)(2,1)} %bitcast.20, bf16[128,3584]{1,0:T(8,128)(2,1)} %bitcast.21, bf16[128,3584]{1,0:T(8,128)(2,1)} %bitcast.22, s32[2,128]{1,0:T(2,128)} %bitcast.26, s32[2,128]{1,0:T(2,128)} %bitcast.27, bf16[1,3584]{1,0:T(2,128)(2,1)} %gain_hbm.1, ...), custom_call_target="tpu_custom_call" | custom-call | flops 18790481920 | bytes 30000000 | tf_op jit(solution)/shard_map/layer/pallas_call | solution.py:500
  153.3 2.4 %leave.1 = (bf16[128,3584]{1,0:T(8,128)(2,1)}, bf16[128,3584]{1,0:T(8,128)(2,1)}) custom-call(bf16[128,3584]{1,0:T(8,128)(2,1)} %get-tuple-element.6.f_hbm, bf16[128,3584]{1,0:T(8,128)(2,1)} %get-tuple-element.7.b_hbm), custom_call_target="tpu_custom_call" | custom-call | bytes 3670016 | tf_op jit(solution)/shard_map/leave/pallas_call | solution.py:515

commit v4 on v3

--- a/solution.py
+++ b/solution.py
@@ -22,6 +22,8 @@
 NONE = -1000.0
 XS = 4
 QUARTER = T // XS
+TURNS = (1, 3, 2, 0)
+SPANS = {5: (0, 3 * MAIN), 6: (3 * MAIN, 2 * MAIN)}
 
 
 def nt(a, b):
@@ -81,7 +83,7 @@
     fwd_hbm, saved_hbm, cot_hbm, idf_hbm, idb_hbm, gain_hbm, router_hbm, wg_hbm, wu_hbm, wd_hbm,
     of_hbm, ob_hbm,
     wg, wu, wd, a1s, a1r, a2s, a2r, a3s, a3r, r1r, r2r, ps, pr,
-    xr, cr, saved, normed, arr_f, arr_b, dg, du, gates_b, ups_b, scaled, router, gain,
+    xr, saved, normed, arr_f, arr_b, dg, du, gates_b, ups_b, scaled, router, gain,
     idf, idb, rowf, rowb, colf, colb, gf, gb,
     via, ssem, rsem, hsend, hrecv, vsend, vrecv, lsem, osem,
 ):
@@ -169,37 +171,37 @@
             def _():
                 onward(n, j).wait_send()
 
-    def near_peer(i):
-        return near + (zed + i // 2 + 1) % 4 * 2 + (core + i + 1) % 2
-
-    def far_peer(i):
-        return far + (zed + 2 + i // 2 * 3) % 4 * 2 + (core + i) % 2
-
-    def near_from(i):
-        return near + (zed + 3 - i // 2) % 4 * 2 + (core + i + 1) % 2
-
-    def far_from(i):
-        return far + (zed + 2 + i // 2) % 4 * 2 + (core + i) % 2
+    def peer(half, dz, dc):
+        return half + (zed + dz) % 4 * 2 + (core + dc) % 2
 
     def remote(k, src, dst, p, at):
+        first, count = SPANS.get(k, (0, src.shape[1]))
+        span = pl.ds(first, count)
         return pltpu.make_async_remote_copy(
-            src.at[p], dst.at[at], ssem.at[k, p], rsem.at[k, at], device_id=(s, p), device_id_type=MESH)
+            src.at[p, span], dst.at[at, span], ssem.at[k, p], rsem.at[k, at], device_id=(s, p), device_id_type=MESH)
 
     def own(k, src, dst):
-        return pltpu.make_async_copy(src.at[e], dst.at[e], rsem.at[k, e])
-
-    def each(count, act):
-        def step(i, _):
-            act(i)
+        first, count = SPANS.get(k, (0, src.shape[1]))
+        span = pl.ds(first, count)
+        return pltpu.make_async_copy(src.at[e, span], dst.at[e, span], rsem.at[k, e])
+
+    def others(act):
+        def step(d, _):
+            act((e + d) % E)
             return 0
 
-        lax.fori_loop(0, count, step, 0)
+        lax.fori_loop(1, E, step, 0)
 
     def send_far(k, src, dst):
-        each(HALF, lambda i: remote(k, src, dst, far_peer(i), e).start())
+        for dc in (0, 1):
+            for dz in TURNS:
+                remote(k, src, dst, peer(far, dz, dc), e).start()
 
     def send_near(k, src, dst):
-        each(HALF - 1, lambda i: remote(k, src, dst, near_peer(i), e).start())
+        for dc in (1, 0):
+            for dz in TURNS:
+                if (dz, dc) != (0, 0):
+                    remote(k, src, dst, peer(near, dz, dc), e).start()
         own(k, src, dst).start()
 
     def send(k, src, dst):
@@ -207,19 +209,11 @@
         send_near(k, src, dst)
 
     def arrive(k, src, dst):
-        def wait(p):
-            remote(k, src, dst, p, p).wait_recv()
-
-        each(HALF - 1, lambda i: wait(near_from(i)))
-        each(HALF, lambda i: wait(far_from(i)))
+        others(lambda p: remote(k, src, dst, p, p).wait_recv())
         own(k, src, dst).wait()
 
     def sent(k, src, dst):
-        def wait(p):
-            remote(k, src, dst, p, e).wait_send()
-
-        each(HALF - 1, lambda i: wait(near_peer(i)))
-        each(HALF, lambda i: wait(far_peer(i)))
+        others(lambda p: remote(k, src, dst, p, e).wait_send())
 
     def norm(x_ref, by, out):
         x = x_ref[...].astype(F32)
@@ -233,7 +227,7 @@
 
         def step(q, _):
             got = nn(main, x_ref[:, pl.ds(pl.multiple_of(q * WIDE, 128), WIDE)]).astype(BF16)
-            buf[pl.ds(first, HALF), pl.ds(pl.multiple_of(q * MAIN, MAIN), MAIN), :] = got.reshape(HALF, MAIN, WIDE)
+            buf[pl.ds(first, HALF), pl.ds(pl.multiple_of(q * MAIN + MAIN, MAIN), MAIN), :] = got.reshape(HALF, MAIN, WIDE)
             return 0
 
         lax.fori_loop(0, PARTS, step, 0)
@@ -241,7 +235,7 @@
             nn(picks(rows, (2, 3), base, float(OVER * q)), x_ref[:, q * WIDE : (q + 1) * WIDE])
             for q in range(PARTS)
         )
-        buf[pl.ds(first, HALF), MAIN * PARTS : BLOCK, :] = over.astype(BF16).reshape(HALF, MAIN, WIDE)
+        buf[pl.ds(first, HALF), 0:MAIN, :] = over.astype(BF16).reshape(HALF, MAIN, WIDE)
 
     def dispatch(k, x_ref, rows, src, dst):
         pack(x_ref, rows, src, far)
@@ -250,12 +244,12 @@
         send_near(k, src, dst)
 
     def unpack(buf, out):
-        tail = buf[:, MAIN * PARTS : BLOCK, :].reshape(E * MAIN, WIDE)
+        tail = buf[:, 0:MAIN, :].reshape(E * MAIN, WIDE)
         row, lane = iota((E * OVER, E * MAIN), 0), iota((E * OVER, E * MAIN), 1)
 
         def step(q, _):
             columns = pl.ds(pl.multiple_of(q * WIDE, 128), WIDE)
-            out[0 : E * MAIN, columns] = buf[:, pl.ds(pl.multiple_of(q * MAIN, MAIN), MAIN), :].reshape(E * MAIN, WIDE)
+            out[0 : E * MAIN, columns] = buf[:, pl.ds(pl.multiple_of(q * MAIN + MAIN, MAIN), MAIN), :].reshape(E * MAIN, WIDE)
             pick = (lane == (row // OVER) * MAIN + OVER * q + row % OVER).astype(BF16)
             out[E * MAIN : ROWS, columns] = nn(pick, tail).astype(BF16)
             return 0
@@ -264,27 +258,25 @@
 
     def lay(q, buf, value):
         low = value.astype(BF16)
-        buf[:, pl.ds(pl.multiple_of(q * MAIN, MAIN), MAIN), :] = low[0 : E * MAIN].reshape(E, MAIN, WIDE)
+        buf[:, pl.ds(pl.multiple_of(q * MAIN + MAIN, MAIN), MAIN), :] = low[0 : E * MAIN].reshape(E, MAIN, WIDE)
         row, lane = iota((E * MAIN, E * OVER), 0), iota((E * MAIN, E * OVER), 1)
         here = (lane == (row // MAIN) * OVER + row % OVER) & (row % MAIN // OVER == q)
         return nn(here.astype(BF16), low[E * MAIN : ROWS])
 
     scope = jax.named_scope
-    with scope("start"):
-        loads[1].wait()
-        rowb[...] = route(idb[...])
-        loads[3].wait()
-        rowf[...] = route(idf[...])
-        loads[0].wait()
-        loads[2].wait()
-        gb[:, 0:1] = norm(saved, gain, normed)
     with scope("barrier"):
         pl.semaphore_wait(barrier, E - 1 + layers - 1)
-    with scope("rows_b_out"):
         hop(1)
         hop(0)
         for load in loads[4:]:
             load.start()
+    with scope("start"):
+        loads[1].wait()
+        rowb[...] = route(idb[...])
+        loads[0].wait()
+        loads[2].wait()
+        gb[:, 0:1] = norm(saved, gain, normed)
+    with scope("rows_b_out"):
         dispatch(0, normed, rowb, a1s, a1r)
     with scope("gating_b"):
         colb[...] = stand(rowb[...])
@@ -292,6 +284,8 @@
         score, total, weight = gates(nt(normed[...], router[...]), colb)
         gb[:, 1:2], gb[:, 2:3], gb[:, 3:4] = score[0], score[1], total
         gb[:, 4:5], gb[:, 5:6] = weight[0], weight[1]
+        loads[3].wait()
+        rowf[...] = route(idf[...])
     with scope("relay"):
         relay(1)
         relay(0)
@@ -327,7 +321,7 @@
     def hidden(n, prod):
         columns = pl.ds(pl.multiple_of(n * HTILE, HTILE), HTILE)
         gate, up = gates_b[:, columns], ups_b[:, columns]
-        grad = nt(cr[...], wd[columns, :])
+        grad = nt(xr[...], wd[columns, :])
         sig = jax.nn.sigmoid(gate)
         act = (gate * sig * up).astype(BF16).astype(F32)
         dg[:, columns] = (grad * up * sig * (1.0 + gate * (1.0 - sig))).astype(BF16)
@@ -335,7 +329,7 @@
         return prod + jnp.sum(act * grad, axis=1, keepdims=True)
 
     with scope("hidden_b"):
-        unpack(a2r, cr)
+        unpack(a2r, xr)
         prod = lax.fori_loop(0, H // HTILE, hidden, jnp.zeros((ROWS, 1), F32))
     prod = jnp.broadcast_to(prod, (ROWS, T)).astype(BF16)
     ps[:, 0:MAIN, :] = prod[0 : E * MAIN].reshape(E, MAIN, T)
@@ -352,7 +346,7 @@
 
     with scope("unit_b"):
         over = lax.fori_loop(0, PARTS, unit, jnp.zeros((E * MAIN, WIDE), F32))
-    a1s[:, MAIN * PARTS : BLOCK, :] = over.astype(BF16).reshape(E, MAIN, WIDE)
+    a1s[:, 0:MAIN, :] = over.astype(BF16).reshape(E, MAIN, WIDE)
     send(4, a1s, r1r)
 
     with scope("wait_rows_f"):
@@ -376,8 +370,9 @@
 
     with scope("down_f"):
         over = lax.fori_loop(0, PARTS, down, jnp.zeros((E * MAIN, WIDE), F32))
-    a2s[:, MAIN * PARTS : BLOCK, :] = over.astype(BF16).reshape(E, MAIN, WIDE)
+    a2s[:, 0:MAIN, :] = over.astype(BF16).reshape(E, MAIN, WIDE)
     send(5, a2s, r2r)
+    send(6, a2s, r2r)
 
     with scope("wait_unit"):
         arrive(3, ps, pr)
@@ -404,8 +399,8 @@
     def grad_in(q, dot):
         columns = pl.ds(pl.multiple_of(q * WIDE, 128), WIDE)
         over_w = spread(places[2:4], weight, (OVER * q).astype(F32))
-        got = nn(main_w, r1r[:, pl.ds(pl.multiple_of(q * MAIN, MAIN), MAIN), :].reshape(E * MAIN, WIDE))
-        got += nn(over_w, r1r[:, MAIN * PARTS : BLOCK, :].reshape(E * MAIN, WIDE))
+        got = nn(main_w, r1r[:, pl.ds(pl.multiple_of(q * MAIN + MAIN, MAIN), MAIN), :].reshape(E * MAIN, WIDE))
+        got += nn(over_w, r1r[:, 0:MAIN, :].reshape(E * MAIN, WIDE))
         got += nn(dlogits, router[:, columns])
         got *= gain[:, columns].astype(F32)
         scaled[:, columns] = got
@@ -425,25 +420,27 @@
         lax.fori_loop(0, PARTS, finish_b, 0)
     out_b = pltpu.make_async_copy(saved, ob_hbm, osem.at[0])
     out_b.start()
+    halves = [pl.ds(i * (D // 2), D // 2) for i in (0, 1)]
+    out_f = [pltpu.make_async_copy(normed.at[:, half], of_hbm.at[:, half], osem.at[1 + i]) for i, half in enumerate(halves)]
 
     places_f = [colf[:, p : p + 1] for p in range(4)]
     weight_f = [gf[:, 0:1], gf[:, 1:2]]
     main_f = spread(places_f[0:2], weight_f, 0.0)
-    with scope("wait_out_f"):
-        arrive(5, a2s, r2r)
-
     def finish_f(q, _):
         columns = pl.ds(pl.multiple_of(q * WIDE, 128), WIDE)
         over_w = spread(places_f[2:4], weight_f, (OVER * q).astype(F32))
-        got = nn(main_f, r2r[:, pl.ds(pl.multiple_of(q * MAIN, MAIN), MAIN), :].reshape(E * MAIN, WIDE))
-        got += nn(over_w, r2r[:, MAIN * PARTS : BLOCK, :].reshape(E * MAIN, WIDE))
+        got = nn(main_f, r2r[:, pl.ds(pl.multiple_of(q * MAIN + MAIN, MAIN), MAIN), :].reshape(E * MAIN, WIDE))
+        got += nn(over_w, r2r[:, 0:MAIN, :].reshape(E * MAIN, WIDE))
         normed[:, columns] = (arr_f[:, columns].astype(F32) + got).astype(BF16)
         return 0
 
     with scope("finish_f"):
-        lax.fori_loop(0, PARTS, finish_f, 0)
-    out_f = pltpu.make_async_copy(normed, of_hbm, osem.at[1])
-    out_f.start()
+        arrive(5, a2s, r2r)
+        lax.fori_loop(0, PARTS // 2, finish_f, 0)
+        out_f[0].start()
+        arrive(6, a2s, r2r)
+        lax.fori_loop(PARTS // 2, PARTS, finish_f, 0)
+        out_f[1].start()
     with scope("drain"):
         hop_sent(0)
         hop_sent(1)
@@ -451,8 +448,10 @@
         sent(3, ps, pr)
         sent(4, a1s, r1r)
         sent(5, a2s, r2r)
+        sent(6, a2s, r2r)
         out_b.wait()
-        out_f.wait()
+        out_f[0].wait()
+        out_f[1].wait()
 
 
 def leave(f_hbm, b_hbm, of_hbm, ob_hbm, f_ref, b_ref, in_sem, out_sem):
@@ -482,7 +481,7 @@
         vm(D, H), vm(D, H), vm(H, D),
         *[vm(*block) for _ in range(8)],
         vm(E, 2 * MAIN, T), vm(E, 2 * MAIN, T),
-        vm(ROWS, D), vm(ROWS, D),
+        vm(ROWS, D),
         *[vm(T, D) for _ in range(4)],
         vm(ROWS, H), vm(ROWS, H), vm(ROWS, H, dtype=F32), vm(ROWS, H, dtype=F32),
         vm(T, D, dtype=F32),
@@ -491,17 +490,17 @@
         *[vm(8, T, dtype=F32) for _ in range(2)],
         *[vm(T, T, dtype=F32) for _ in range(4)],
         vm(2, QUARTER, D),
-        pltpu.SemaphoreType.DMA((6, E)), pltpu.SemaphoreType.DMA((6, E)),
+        pltpu.SemaphoreType.DMA((7, E)), pltpu.SemaphoreType.DMA((7, E)),
         pltpu.SemaphoreType.DMA((2, XS)), pltpu.SemaphoreType.DMA((2, XS)),
         pltpu.SemaphoreType.DMA((2,)), pltpu.SemaphoreType.DMA((2,)),
-        pltpu.SemaphoreType.DMA((8,)), pltpu.SemaphoreType.DMA((2,)),
+        pltpu.SemaphoreType.DMA((8,)), pltpu.SemaphoreType.DMA((3,)),
     ]
     out = jax.ShapeDtypeStruct((T, D), BF16)
     fwd_out, bwd_grad = pl.pallas_call(
         kernel,
         out_shape=(out, out),
-        in_specs=[pl.BlockSpec(memory_space=pl.ANY)] * 10,
-        out_specs=(pl.BlockSpec(memory_space=pl.ANY),) * 2,
+        in_specs=[pl.BlockSpec(memory_space=pltpu.HBM)] * 10,
+        out_specs=(pl.BlockSpec(memory_space=pltpu.HBM),) * 2,
         scratch_shapes=scratch,
         name="layer",
         compiler_params=pltpu.CompilerParams(
@@ -515,8 +514,8 @@
     fwd_out, bwd_grad = pl.pallas_call(
         leave,
         out_shape=(out, out),
-        in_specs=[pl.BlockSpec(memory_space=pl.ANY)] * 2,
-        out_specs=(pl.BlockSpec(memory_space=pl.ANY),) * 2,
+        in_specs=[pl.BlockSpec(memory_space=pltpu.HBM)] * 2,
+        out_specs=(pl.BlockSpec(memory_space=pltpu.HBM),) * 2,
         scratch_shapes=[vm(T, D), vm(T, D), pltpu.SemaphoreType.DMA((2, 4)), pltpu.SemaphoreType.DMA((2, 4))],
         name="leave",
         cost_estimate=pl.CostEstimate(flops=0, bytes_accessed=4 * 2 * T * D, transcendentals=0),

time: 157 us -> 153 us (0.975)
  Pallas kernels: 155 us -> 152 us
    pallas_call x1, Pallas kernels: 153 us -> 149 us  [per_device(): pl.pallas_call(kernel, out_shape=(out, out), in_specs=[pl.BlockSpec(memor...]
where the time goes in v4:
time: 153 us
  Pallas kernels  152 us (99%)
    pallas_call x1, Pallas kernels, per_device(): pl.pallas_call(kernel, out_shape=(out, out), in_specs=[pl.BlockSpec(memor...  149 us

profile of v4, /device:TPU:1, one launch (start us, length us, event | category | flops | bytes accessed | tf_op | source)
XLA Modules:
  0.0 152.5 jit_solution(4580936386440237523)
XLA Ops:
  0.6 149.5 %layer.1 = (bf16[128,3584]{1,0:T(8,128)(2,1)}, bf16[128,3584]{1,0:T(8,128)(2,1)}) custom-call(bf16[128,3584]{1,0:T(8,128)(2,1)} %bitcast.20, bf16[128,3584]{1,0:T(8,128)(2,1)} %bitcast.21, bf16[128,3584]{1,0:T(8,128)(2,1)} %bitcast.22, s32[2,128]{1,0:T(2,128)} %bitcast.26, s32[2,128]{1,0:T(2,128)} %bitcast.27, bf16[1,3584]{1,0:T(2,128)(2,1)} %gain_hbm.1, ...), custom_call_target="tpu_custom_call" | custom-call | flops 18790481920 | bytes 30000000 | tf_op jit(solution)/shard_map/layer/pallas_call | solution.py:499
  150.1 2.4 %leave.1 = (bf16[128,3584]{1,0:T(8,128)(2,1)}, bf16[128,3584]{1,0:T(8,128)(2,1)}) custom-call(bf16[128,3584]{1,0:T(8,128)(2,1)} %get-tuple-element.6.f_hbm, bf16[128,3584]{1,0:T(8,128)(2,1)} %get-tuple-element.7.b_hbm), custom_call_target="tpu_custom_call" | custom-call | bytes 3670016 | tf_op jit(solution)/shard_map/leave/pallas_call | solution.py:514

commit v5 on v4

--- a/solution.py
+++ b/solution.py
@@ -139,7 +139,6 @@
             device_id=(band * XS + ways[n][0], e), device_id_type=MESH)
 
     def hop(n):
-        quarter(n, 0).start()
         for j in range(1, XS):
 
             @pl.when(at_end[n])
@@ -149,6 +148,8 @@
             @pl.when(jnp.logical_not(at_end[n]))
             def _():
                 quarter(n, j).start()
+
+        quarter(n, 0).start()
 
     def relay(n):
         for j in range(1, XS):
@@ -264,20 +265,23 @@
         return nn(here.astype(BF16), low[E * MAIN : ROWS])
 
     scope = jax.named_scope
-    with scope("barrier"):
-        pl.semaphore_wait(barrier, E - 1 + layers - 1)
-        hop(1)
-        hop(0)
-        for load in loads[4:]:
-            load.start()
     with scope("start"):
         loads[1].wait()
         rowb[...] = route(idb[...])
         loads[0].wait()
         loads[2].wait()
         gb[:, 0:1] = norm(saved, gain, normed)
+        pack(normed, rowb, a1s, far)
+    with scope("barrier"):
+        pl.semaphore_wait(barrier, E - 1 + layers - 1)
     with scope("rows_b_out"):
-        dispatch(0, normed, rowb, a1s, a1r)
+        hop(1)
+        hop(0)
+        send_far(0, a1s, a1r)
+        pack(normed, rowb, a1s, near)
+        send_near(0, a1s, a1r)
+        for load in loads[4:]:
+            load.start()
     with scope("gating_b"):
         colb[...] = stand(rowb[...])
         loads[4].wait()
@@ -332,10 +336,11 @@
         unpack(a2r, xr)
         prod = lax.fori_loop(0, H // HTILE, hidden, jnp.zeros((ROWS, 1), F32))
     prod = jnp.broadcast_to(prod, (ROWS, T)).astype(BF16)
-    ps[:, 0:MAIN, :] = prod[0 : E * MAIN].reshape(E, MAIN, T)
     row, lane = iota((E * MAIN, E * OVER), 0), iota((E * MAIN, E * OVER), 1)
     here = (lane == (row // MAIN) * OVER + row % OVER).astype(BF16)
-    ps[:, MAIN : 2 * MAIN, :] = nn(here, prod[E * MAIN : ROWS]).astype(BF16).reshape(E, MAIN, T)
+    over = nn(here, prod[E * MAIN : ROWS]).astype(BF16)
+    side = iota((E * MAIN, T), 1) < T // 2
+    ps[...] = jnp.where(side, prod[0 : E * MAIN].astype(F32), over.astype(F32)).astype(BF16).reshape(E, MAIN, T)
     send(3, ps, pr)
     with scope("wait_rows_b_sent"):
         sent(0, a1s, a1r)
@@ -384,9 +389,9 @@
     one = jnp.ones((T, 1), F32)
     product = []
     for k in (0, 1):
-        got = nn(spread([places[k]], [one], 0.0), pr[:, 0:MAIN, :].reshape(E * MAIN, T))
-        got += nn(spread([places[2 + k]], [one], 0.0), pr[:, MAIN : 2 * MAIN, :].reshape(E * MAIN, T))
-        product.append(got[:, 0:1])
+        main = nn(spread([places[k]], [one], 0.0), pr[...].reshape(E * MAIN, T))[:, 0:1]
+        over = nn(spread([places[2 + k]], [one], 0.0), pr[...].reshape(E * MAIN, T))[:, T // 2 : T // 2 + 1]
+        product.append(main + over)
     mixed = (product[0] * weight[0] + product[1] * weight[1]) * (1.0 / route_scale)
     lanes = iota((T, E), 1).astype(F32)
     dlogits = jnp.zeros((T, E), F32)
@@ -420,8 +425,8 @@
         lax.fori_loop(0, PARTS, finish_b, 0)
     out_b = pltpu.make_async_copy(saved, ob_hbm, osem.at[0])
     out_b.start()
-    halves = [pl.ds(i * (D // 2), D // 2) for i in (0, 1)]
-    out_f = [pltpu.make_async_copy(normed.at[:, half], of_hbm.at[:, half], osem.at[1 + i]) for i, half in enumerate(halves)]
+    pieces = [pl.ds(i * (D // 2), D // 2) for i in (0, 1)]
+    out_f = [pltpu.make_async_copy(normed.at[:, piece], of_hbm.at[:, piece], osem.at[1 + i]) for i, piece in enumerate(pieces)]
 
     places_f = [colf[:, p : p + 1] for p in range(4)]
     weight_f = [gf[:, 0:1], gf[:, 1:2]]
@@ -480,7 +485,7 @@
     scratch = [
         vm(D, H), vm(D, H), vm(H, D),
         *[vm(*block) for _ in range(8)],
-        vm(E, 2 * MAIN, T), vm(E, 2 * MAIN, T),
+        vm(E, MAIN, T), vm(E, MAIN, T),
         vm(ROWS, D),
         *[vm(T, D) for _ in range(4)],
         vm(ROWS, H), vm(ROWS, H), vm(ROWS, H, dtype=F32), vm(ROWS, H, dtype=F32),

time: 153 us -> 152 us (level)
  no operation moved by 1% of the time
where the time goes in v5:
time: 152 us
  Pallas kernels  151 us (99%)
    pallas_call x1, Pallas kernels, per_device(): pl.pallas_call(kernel, out_shape=(out, out), in_specs=[pl.BlockSpec(memor...  149 us

profile of v5, /device:TPU:1, one launch (start us, length us, event | category | flops | bytes accessed | tf_op | source)
XLA Modules:
  0.0 151.8 jit_solution(18353557259988349520)
XLA Ops:
  0.6 148.8 %layer.1 = (bf16[128,3584]{1,0:T(8,128)(2,1)}, bf16[128,3584]{1,0:T(8,128)(2,1)}) custom-call(bf16[128,3584]{1,0:T(8,128)(2,1)} %bitcast.20, bf16[128,3584]{1,0:T(8,128)(2,1)} %bitcast.21, bf16[128,3584]{1,0:T(8,128)(2,1)} %bitcast.22, s32[2,128]{1,0:T(2,128)} %bitcast.26, s32[2,128]{1,0:T(2,128)} %bitcast.27, bf16[1,3584]{1,0:T(2,128)(2,1)} %gain_hbm.1, ...), custom_call_target="tpu_custom_call" | custom-call | flops 18790481920 | bytes 30000000 | tf_op jit(solution)/shard_map/layer/pallas_call | solution.py:504
  149.4 2.4 %leave.1 = (bf16[128,3584]{1,0:T(8,128)(2,1)}, bf16[128,3584]{1,0:T(8,128)(2,1)}) custom-call(bf16[128,3584]{1,0:T(8,128)(2,1)} %get-tuple-element.6.f_hbm, bf16[128,3584]{1,0:T(8,128)(2,1)} %get-tuple-element.7.b_hbm), custom_call_target="tpu_custom_call" | custom-call | bytes 3670016 | tf_op jit(solution)/shard_map/leave/pallas_call | solution.py:519

commit v6 on v5

--- a/solution.py
+++ b/solution.py
@@ -282,6 +282,9 @@
         send_near(0, a1s, a1r)
         for load in loads[4:]:
             load.start()
+    with scope("relay"):
+        relay(1)
+        relay(0)
     with scope("gating_b"):
         colb[...] = stand(rowb[...])
         loads[4].wait()
@@ -290,9 +293,6 @@
         gb[:, 4:5], gb[:, 5:6] = weight[0], weight[1]
         loads[3].wait()
         rowf[...] = route(idf[...])
-    with scope("relay"):
-        relay(1)
-        relay(0)
     with scope("wait_hop_b"):
         hop_arrive(1)
     with scope("cot_near_out"):

time: 152 us -> 152 us (level)
  no operation moved by 1% of the time
where the time goes in v6:
time: 152 us
  Pallas kernels  151 us (99%)
    pallas_call x1, Pallas kernels, per_device(): pl.pallas_call(kernel, out_shape=(out, out), in_specs=[pl.BlockSpec(memor...  149 us

profile of v6, /device:TPU:1, one launch (start us, length us, event | category | flops | bytes accessed | tf_op | source)
XLA Modules:
  0.0 151.8 jit_solution(7732416738923023235)
XLA Ops:
  0.6 148.8 %layer.1 = (bf16[128,3584]{1,0:T(8,128)(2,1)}, bf16[128,3584]{1,0:T(8,128)(2,1)}) custom-call(bf16[128,3584]{1,0:T(8,128)(2,1)} %bitcast.20, bf16[128,3584]{1,0:T(8,128)(2,1)} %bitcast.21, bf16[128,3584]{1,0:T(8,128)(2,1)} %bitcast.22, s32[2,128]{1,0:T(2,128)} %bitcast.26, s32[2,128]{1,0:T(2,128)} %bitcast.27, bf16[1,3584]{1,0:T(2,128)(2,1)} %gain_hbm.1, ...), custom_call_target="tpu_custom_call" | custom-call | flops 18790481920 | bytes 30000000 | tf_op jit(solution)/shard_map/layer/pallas_call | solution.py:504
  149.4 2.4 %leave.1 = (bf16[128,3584]{1,0:T(8,128)(2,1)}, bf16[128,3584]{1,0:T(8,128)(2,1)}) custom-call(bf16[128,3584]{1,0:T(8,128)(2,1)} %get-tuple-element.6.f_hbm, bf16[128,3584]{1,0:T(8,128)(2,1)} %get-tuple-element.7.b_hbm), custom_call_target="tpu_custom_call" | custom-call | bytes 3670016 | tf_op jit(solution)/shard_map/leave/pallas_call | solution.py:519
